TPU v7x, 128 devices: a whole 4x4x4 slice. The times are simulated.
128 devices in a mesh: side: 4 (over z_hi, core), dev: 32 (over z_lo, x, y).
Axes of the slice: x: 4, y: 4, z: 4 (z_hi: 2, z_lo: 2; z = z_hi * 2 + z_lo), core: 2. Of those that a mesh axis runs over, the one named last changes fastest.
Arguments:
- query: bfloat16 [4, 32, 8, 4096], P('side', 'dev'), may hold values from -20 to 20, as said below
- new_key: bfloat16 [4, 32, 8, 1024], P('side', 'dev'), may hold values from -6 to 6
- new_value: bfloat16 [4, 32, 8, 1024], P('side', 'dev'), may hold values from -6 to 6
- cache_key: bfloat16 [4, 32, 8, 128, 1024], P('side', 'dev'), may hold values from -20 to 20, as said below
- cache_value: bfloat16 [4, 32, 8, 128, 1024], P('side', 'dev'), may hold values from -6 to 6
- lengths: int32 [4, 32, 8], P('side', 'dev'), may hold values from 2 to 128, as said below
- residual: bfloat16 [4, 32, 8, 4096], P('side', 'dev'), may hold values from -6 to 6
- norm_gain: float32 [4096], replicated, may hold values from 0.1 to 1.9
- router_weight: bfloat16 [4096, 4], replicated, may hold values from -0.09375 to 0.09375
- gate_weight: bfloat16 [4, 4096, 28672], P('side', None, 'dev'), may hold values from -0.09375 to 0.09375
- up_weight: bfloat16 [4, 4096, 28672], P('side', None, 'dev'), may hold values from -0.09375 to 0.09375
- down_weight: bfloat16 [4, 28672, 4096], P('side', 'dev'), may hold values from -0.0625 to 0.0625
- slot_rows: int32 [4, 32, 4, 8], P('side', 'dev'), may hold values from 0 to 7, as said below
- slot_count: int32 [4, 32, 4], P('side', 'dev'), may hold values from 0 to 8, as said below
Outputs:
- layer_out: bfloat16 [4, 32, 8, 4096], P('side', 'dev')
Inputs may be any that keep to these rules, and one draw needn't show every extreme that they name: query: without structure in the shown draw. cache_key: without structure in the shown draw. `lengths`: row (0, 0, 0) has length 128. `slot_rows`: each row stands in exactly two lists of its device, at most once in each; the used slots list rows in ascending order; one expert, drawn from the seed, has every row of every device in its lists; unused slots hold arbitrary rows. `slot_count`: the counts of one device sum to 16.
All inputs are finite; a program needn't handle non-finite values.
Results may differ from a plain program's by a relative error of at most 0.012.
Values may be sent and summed in bfloat16 or wider, within the bound.
A program may use at most 128 MiB of HBM per device.

v0:
```python
import math

import jax
import jax.numpy as jnp
from jax import lax
from jax.sharding import PartitionSpec as P

HEADS = 32
KVH = 8
HD = 128


def spread(value, axis, source):
    kept = jnp.where(lax.axis_index(axis) == source, value, 0).astype(value.dtype)
    return lax.psum(kept, axis)


def attend(query, new_key, new_value, cache_key, cache_value, lengths):
    row_count = query.shape[0]
    context_len = cache_key.shape[1]
    group_size = HEADS // KVH
    queries = query.reshape(row_count, KVH, group_size, HD)
    keys_all = cache_key.reshape(row_count, context_len, KVH, HD)
    values_all = cache_value.reshape(row_count, context_len, KVH, HD)
    score_scale = 1.0 / math.sqrt(HD)
    scores = (
        jnp.einsum("rkgd,rckd->rkgc", queries, keys_all, preferred_element_type=jnp.float32)
        * score_scale
    )
    own_score = (
        jnp.einsum(
            "rkgd,rkd->rkg",
            queries,
            new_key.reshape(row_count, KVH, HD),
            preferred_element_type=jnp.float32,
        )
        * score_scale
    )
    visible = jnp.arange(context_len, dtype=jnp.int32)[None, :] < lengths[:, None]
    scores = jnp.where(visible[:, None, None, :], scores, -jnp.inf)
    row_top = jnp.maximum(jnp.max(scores, axis=3), own_score)
    probs = jnp.exp(scores - row_top[..., None])
    own_prob = jnp.exp(own_score - row_top)
    denominator = jnp.sum(probs, axis=3) + own_prob
    weights = (probs / denominator[..., None]).astype(jnp.bfloat16)
    own_weight = (own_prob / denominator).astype(jnp.bfloat16)
    context = jnp.einsum("rkgc,rckd->rkgd", weights, values_all, preferred_element_type=jnp.float32)
    context = context + own_weight.astype(jnp.float32)[..., None] * new_value.reshape(
        row_count, KVH, 1, HD
    ).astype(jnp.float32)
    return context.reshape(row_count, HEADS * HD)


def local(
    query,
    new_key,
    new_value,
    cache_key,
    cache_value,
    lengths,
    residual,
    norm_gain,
    router_weight,
    gate_weight,
    up_weight,
    down_weight,
    slot_rows,
    slot_count,
):
    pod_count = lax.axis_size("side") - 1
    device_count = lax.axis_size("dev")
    expert_count = router_weight.shape[1]
    shard_count = device_count // expert_count
    width = residual.shape[3]
    side_index = lax.axis_index("side")
    pod_index = jnp.minimum(side_index, pod_count - 1)
    row_count = query.shape[2]
    capacity = slot_rows.shape[3]
    gate_local = gate_weight[0]
    up_local = up_weight[0]
    down_local = down_weight[0]
    context = attend(
        query[0, 0],
        new_key[0, 0],
        new_value[0, 0],
        cache_key[0, 0],
        cache_value[0, 0],
        lengths[0, 0],
    )
    stream = residual[0, 0].astype(jnp.float32) + context
    normed = (
        stream * lax.rsqrt(jnp.mean(stream * stream, axis=1, keepdims=True) + 1e-05) * norm_gain
    ).astype(jnp.bfloat16)
    logits = jnp.dot(normed, router_weight, preferred_element_type=jnp.float32)
    listed = slot_rows[0, 0]
    counted = slot_count[0, 0]
    row_ids = jnp.arange(row_count, dtype=jnp.int32)
    slot_ids = jnp.arange(capacity, dtype=jnp.int32)
    select = (
        (listed[:, :, None] == row_ids[None, None, :])
        & (slot_ids[None, :, None] < counted[:, None, None])
    ).astype(jnp.float32)
    chosen = jnp.transpose(jnp.sum(select, axis=1))
    raised = chosen * jnp.exp(logits)
    route_weight = raised / jnp.sum(raised, axis=1, keepdims=True)
    outgoing = jnp.einsum(
        "ecr,rd->ecd", select.astype(jnp.bfloat16), normed, preferred_element_type=jnp.float32
    ).astype(jnp.bfloat16)

    def expert_rows(flat_rows):
        gate_value = jnp.dot(flat_rows, gate_local, preferred_element_type=jnp.float32)
        up_value = jnp.dot(flat_rows, up_local, preferred_element_type=jnp.float32)
        hidden = (jax.nn.silu(gate_value) * up_value).astype(jnp.bfloat16)
        return jnp.dot(hidden, down_local, preferred_element_type=jnp.float32)

    def empty_rows(flat_rows):
        return jnp.zeros(flat_rows.shape, jnp.float32)

    arrived = lax.all_gather(outgoing[:, None], "side", axis=1, tiled=True)[:, :pod_count]
    sectioned = jnp.broadcast_to(arrived[:, None], (expert_count, shard_count) + arrived.shape[1:])
    sectioned = sectioned.reshape((device_count,) + arrived.shape[1:])
    expert_batch = lax.all_to_all(sectioned, "dev", split_axis=0, concat_axis=0, tiled=True)
    flat_rows = expert_batch.reshape(-1, width)
    result = lax.cond(side_index == pod_count, expert_rows, empty_rows, flat_rows)
    partial_value = result.reshape(expert_batch.shape)
    returned = lax.all_to_all(
        partial_value.astype(jnp.bfloat16), "dev", split_axis=0, concat_axis=0, tiled=True
    ).astype(partial_value.dtype)
    summed = jnp.sum(
        returned.reshape((expert_count, shard_count) + returned.shape[1:]), axis=1
    ).astype(jnp.bfloat16)
    pod_outputs = spread(summed, "side", pod_count)
    produced = lax.dynamic_index_in_dim(pod_outputs, pod_index, 1, keepdims=False)
    coefficient = (select * jnp.transpose(route_weight)[:, None, :]).reshape(-1, row_count)
    expert_mix = jnp.dot(
        jnp.transpose(coefficient),
        produced.reshape(-1, width).astype(jnp.float32),
        precision=lax.Precision.HIGHEST,
    ).astype(jnp.bfloat16)
    finished = (stream + expert_mix.astype(jnp.float32)).astype(jnp.bfloat16)
    finished = jnp.where(side_index < pod_count, finished, jnp.zeros_like(finished))
    return finished.reshape(1, 1, row_count, width)


def solution(mesh):
    return jax.shard_map(
        local,
        mesh=mesh,
        in_specs=(
            P("side", "dev", None, None),
            P("side", "dev", None, None),
            P("side", "dev", None, None),
            P("side", "dev", None, None, None),
            P("side", "dev", None, None, None),
            P("side", "dev", None),
            P("side", "dev", None, None),
            P(),
            P(),
            P("side", None, "dev"),
            P("side", None, "dev"),
            P("side", "dev", None),
            P("side", "dev", None, None),
            P("side", "dev", None),
        ),
        out_specs=P("side", "dev", None, None),
        check_vma=False,
    )
```

profile of v0, /device:TPU:1, one launch (start us, length us, event | category | flops | bytes accessed | tf_op | source)
XLA Modules:
  0.0 283.5 jit_solution(18310470604620007275)
XLA Ops:
  6.5 0.9 iota_compare_fusion.2
  7.4 0.7 iota_compare_fusion.1
  8.1 0.7 bitcast_convert_fusion
  8.9 1.0 reshape.179
  9.8 2.2 copy.24
  12.1 1.1 fusion.35
  13.2 2.1 fusion.55
  15.3 0.3 fusion.31
  15.6 0.6 copy.25
  16.3 0.8 multiply_reduce_fusion
  17.3 1.0 convolution_convert_fusion
  18.3 24.7 %all-gather.3.cloned.1.call-done = bf16[4,32,4096]{2,1,0:T(8,128)(2,1)} async-done(((bf16[4,8,4096]{2,1,0:T(8,128)(2,1)}), bf16[4,32,4096]{2,1,0:T(8,128)(2,1)}) %all-gather.3.cloned.1.call-update) | async-done | bytes 1048592 | tf_op jit(solution)/shard_map/all_gather | solution.py:119
  43.0 1.2 slice.4
  44.1 3.4 %broadcast_in_dim.24 = bf16[4,8,3,8,4096]{4,3,2,1,0:T(8,128)(2,1)} broadcast(bf16[4,3,8,4096]{3,2,1,0:T(8,128)(2,1)S(1)} %slice.4), dimensions={0,2,3,4} | broadcast | bytes 7077888 | tf_op jit(solution)/shard_map/broadcast_in_dim | solution.py:120
  47.6 7.0 %all-to-all-start = ((bf16[32,3,8,4096]{3,2,1,0:T(8,128)(2,1)}), bf16[32,3,8,4096]{3,2,1,0:T(8,128)(2,1)}, u32[]{:S(2)}, u32[]{:S(2)}) async-start(bf16[32,3,8,4096]{3,2,1,0:T(8,128)(2,1)} %bitcast.72), calls=%async_computation | async-start | bytes 12582912 | tf_op jit(solution)/shard_map/all_to_all | solution.py:122
  54.7 86.6 %all-to-all-done = bf16[32,3,8,4096]{3,2,1,0:T(8,128)(2,1)} async-done(((bf16[32,3,8,4096]{3,2,1,0:T(8,128)(2,1)}), bf16[32,3,8,4096]{3,2,1,0:T(8,128)(2,1)}, u32[]{:S(2)}, u32[]{:S(2)}) %all-to-all-start) | async-done | bytes 6291488 | tf_op jit(solution)/shard_map/all_to_all | solution.py:122
  141.3 3.4 %conditional.1 = (bf16[768,4096]{1,0:T(8,128)(2,1)}) conditional(s32[]{:T(128)} %convert_element_type.83, () %tuple.11, (bf16[32,3,8,4096]{3,2,1,0:T(8,128)(2,1)}, bf16[1,4096,896]{2,1,0:T(8,128)(2,1)}, bf16[1,4096,896]{2,1,0:T(8,128)(2,1)}, bf16[1,896,4096]{2,1,0:T(8,128)(2,1)}) %tuple.12), branch_computations={%region_5.6_spmd, %region_6.7_spmd} | conditional | flops 16915562496 | bytes 46399496 | solution.py:124
  141.3 3.4 %broadcast.97 = bf16[768,4096]{1,0:T(8,128)(2,1)} broadcast(bf16[]{:T(256)} %constant.88), dimensions={} | broadcast | bytes 6291458 | tf_op jit(solution)/shard_map/broadcast.3
  144.8 82.1 %all_to_all.10 = bf16[32,3,8,4096]{3,2,1,0:T(8,128)(2,1)S(1)} all-to-all(bf16[32,3,8,4096]{3,2,1,0:T(8,128)(2,1)} %bitcast.73), channel_id=1, replica_groups=mesh['side'=4,'dev'=32] {'dev'}, dimensions={0} | all-to-all | bytes 12582912 | tf_op jit(solution)/shard_map/all_to_all | solution.py:126
  226.8 1.1 bitcast_reduce_fusion
  227.9 1.0 broadcast_select_fusion
  229.0 0.2 fusion.51
  229.1 45.6 %all-reduce.2.cloned.1.call-done = bf16[4,3,8,4096]{3,2,1,0:T(8,128)(2,1)} async-done(((bf16[4,3,8,4096]{3,2,1,0:T(8,128)(2,1)}), bf16[4,3,8,4096]{3,2,1,0:T(8,128)(2,1)}) %all-reduce.2.cloned.1.call-update) | async-done | bytes 786448 | tf_op jit(solution)/shard_map/psum | solution.py:15
  274.8 1.9 fusion.15
  (22 shorter events, 0.4 us)
Async XLA Ops:
  6.5 222.4 %copy-start = (bf16[4096,4]{0,1:T(4,128)(2,1)S(1)}, bf16[4096,4]{0,1:T(4,128)(2,1)}, u32[]{:S(2)}) copy-start(bf16[4096,4]{0,1:T(4,128)(2,1)} %param.24) | copy-start | bytes 98308
  6.5 9.1 %copy-start.1 = (bf16[1,1,8,128,1024]{4,3,2,1,0:T(8,128)(2,1)S(1)}, bf16[1,1,8,128,1024]{4,3,2,1,0:T(8,128)(2,1)}, u32[]{:S(2)}) copy-start(bf16[1,1,8,128,1024]{4,3,2,1,0:T(8,128)(2,1)} %param.20) | copy-start | bytes 6291460
  6.5 36.4 %all-gather.3.cloned.1.call-start = ((), (), s32[]{:S(2)}) async-start(), calls=%async_computation.3 | async-start | bytes 1310720 | tf_op jit(solution)/shard_map/all_gather | solution.py:119
  12.1 5.1 %copy-start.2 = (bf16[1,1,8,4096]{3,2,1,0:T(8,128)(2,1)S(1)}, bf16[1,1,8,4096]{3,2,1,0:T(8,128)(2,1)}, u32[]{:S(2)}) copy-start(bf16[1,1,8,4096]{3,2,1,0:T(8,128)(2,1)} %param.22) | copy-start | bytes 196612
  12.1 5.1 %copy-start.4 = (f32[4096]{0:T(1024)S(1)}, f32[4096]{0:T(1024)}, u32[]{:S(2)}) copy-start(f32[4096]{0:T(1024)} %param.23) | copy-start | bytes 49156
  12.1 5.2 %copy-start.3 = (s32[1,1,4,8]{3,2,1,0:T(4,128)S(1)}, s32[1,1,4,8]{3,2,1,0:T(4,128)}, u32[]{:S(2)}) copy-start(s32[1,1,4,8]{3,2,1,0:T(4,128)} %param.28) | copy-start | bytes 388
  47.6 93.7 %all-to-all-start = ((bf16[32,3,8,4096]{3,2,1,0:T(8,128)(2,1)}), bf16[32,3,8,4096]{3,2,1,0:T(8,128)(2,1)}, u32[]{:S(2)}, u32[]{:S(2)}) async-start(bf16[32,3,8,4096]{3,2,1,0:T(8,128)(2,1)} %bitcast.72), calls=%async_computation | async-start | bytes 12582912 | tf_op jit(solution)/shard_map/all_to_all | solution.py:122
  54.6 220.1 %all-reduce.2.cloned.1.call-start = ((), (), s32[]{:S(2)}) async-start(), calls=%async_computation.2 | async-start | bytes 1572864 | tf_op jit(solution)/shard_map/psum | solution.py:15
Sparse Core Ops, SparseCore 0:
  18.4 24.5 all-gather.2
  229.0 45.7 all-reduce.1
where the time goes:
time: 284 us
  waiting for transfers between devices  157 us (55%)
  blocking collectives  82.1 us (29%)
  between operations  13.6 us (5%)
  local copies, waits for them, and re-layouts  11.9 us (4%)
  matrix products  7.09 us (2%)
  starting transfers between devices  7.06 us (2%)
  other arithmetic  4.85 us (2%)
    all_to_all x1, waiting for transfers between devices, local(): lax.all_to_all(sectioned, 'dev', split_axis=0, concat_axis=0, tiled=True)  86.6 us
    all_to_all x1, blocking collectives, local(): lax.all_to_all(partial_value.astype(jnp.bfloat16), 'dev', split_axis=0, c...  82.1 us
    psum x1, waiting for transfers between devices, spread(): return lax.psum(kept, axis)  45.6 us
    all_gather x1, waiting for transfers between devices, local(): lax.all_gather(outgoing[:, None], 'side', axis=1, tiled=True)[:, :pod_count]  24.7 us
    all_to_all x1, starting transfers between devices, local(): lax.all_to_all(sectioned, 'dev', split_axis=0, concat_axis=0, tiled=True)  7.02 us
  transfers between devices with their start and end apart: 3, of which 3 were waited for; matrix products, arithmetic and copies ran while one was open for 0% of the time, Pallas kernels for 0%

commit v1 on v0

v1 whole, which is shorter than its diff:
```python
import functools
import math

import jax
import jax.numpy as jnp
from jax import lax
from jax.experimental import pallas as pl
from jax.experimental.pallas import tpu as pltpu
from jax.sharding import PartitionSpec as P

MESH = pl.DeviceIdType.MESH
F32 = jnp.float32
BF16 = jnp.bfloat16

HD = 128
KVH = 8
GROUP = 4
EXP = 4
ROW = 8
CTX = 128
D = 4096
HALF = D // 2
QUARTER = D // 4
LANES = 128
WIDE = D + LANES
PAY = HALF + LANES
UNITS = 896
TILES = UNITS // LANES
CHUNKS = 3
LEFT, RIGHT = (0, HALF), (HALF, WIDE)
NEG = -1e30


def cols(start, stop):
    return pl.ds(start, stop - start)


def attention(q, nk, nv, ck, cv, lengths, res, gain, router, slot_rows, slot_count, kbuf, vbuf, stream, pay, sems):
    pieces = 4
    wide = KVH * HD // pieces

    def load(source, target, which, piece):
        span = pl.ds(piece * wide, wide)
        return pltpu.make_async_copy(source.at[:, :, span], target.at[:, :, span], sems.at[which, piece])

    for piece in range(pieces):
        load(ck, kbuf, 0, piece).start()
        load(cv, vbuf, 1, piece).start()
    scale = 1.0 / math.sqrt(HD)
    sub = lax.broadcasted_iota(jnp.int32, (ROW, LANES), 0)
    lane = lax.broadcasted_iota(jnp.int32, (ROW, LANES), 1)
    bias = jnp.concatenate(
        [jnp.where((sub == r) & (lane < lengths[0, 0, r]), 0.0, NEG) for r in range(ROW)], axis=1
    ).astype(F32)
    bias = jnp.concatenate([bias] * GROUP, axis=0)
    total = jnp.zeros((ROW, 1), F32)
    for k in range(KVH):
        if k % (KVH // pieces) == 0:
            load(ck, kbuf, 0, k // (KVH // pieces)).wait()
            load(cv, vbuf, 1, k // (KVH // pieces)).wait()
        span = slice(k * HD, (k + 1) * HD)
        heads = [slice((k * GROUP + g) * HD, (k * GROUP + g + 1) * HD) for g in range(GROUP)]
        query = jnp.concatenate([q[0, 0, :, h].astype(F32) for h in heads], axis=0)
        new_key = jnp.concatenate([nk[0, 0, :, span].astype(F32)] * GROUP, axis=0)
        new_value = jnp.concatenate([nv[0, 0, :, span].astype(F32)] * GROUP, axis=0)
        keys = kbuf[:, :, span].reshape(ROW * CTX, HD)
        values = vbuf[:, :, span].reshape(ROW * CTX, HD)
        scores = lax.dot_general(
            query.astype(BF16), keys, (((1,), (1,)), ((), ())), preferred_element_type=F32
        )
        scores = scores * scale + bias
        own = jnp.sum(query * new_key, axis=1, keepdims=True) * scale
        top = jnp.maximum(jnp.max(scores, axis=1, keepdims=True), own)
        probs = jnp.exp(scores - top)
        own_prob = jnp.exp(own - top)
        inverse = 1.0 / (jnp.sum(probs, axis=1, keepdims=True) + own_prob)
        weights = (probs * inverse).astype(BF16)
        own_weight = (own_prob * inverse).astype(BF16).astype(F32)
        context = jnp.dot(weights, values, preferred_element_type=F32) + own_weight * new_value
        for g, h in enumerate(heads):
            part = res[0, 0, :, h].astype(F32) + context[g * ROW : (g + 1) * ROW]
            stream[:, h] = part
            total = total + jnp.sum(part * part, axis=1, keepdims=True)
    rows = stream[...]
    normed = (rows * lax.rsqrt(total / D + 1e-05) * gain[...]).astype(BF16)
    logits = lax.dot_general(normed, router[...], (((1,), (1,)), ((), ())), preferred_element_type=F32)
    raised = []
    for e in range(EXP):
        chosen = jnp.zeros((ROW, 1), F32)
        for c in range(slot_rows.shape[3]):
            hit = (sub[:, 0:1] == slot_rows[0, 0, e, c]) & (c < slot_count[0, 0, e])
            chosen = chosen + jnp.where(hit, 1.0, 0.0)
        raised.append(chosen * jnp.exp(logits[:, e : e + 1]))
    inverse = raised[0] + raised[1] + raised[2] + raised[3]
    table = jnp.zeros((ROW, LANES), F32)
    for e in range(EXP):
        weight = raised[e] / inverse
        high = weight.astype(BF16).astype(F32)
        table = table + jnp.where(lane == e, high, 0.0) + jnp.where(lane == EXP + e, weight - high, 0.0)
    normed = normed.astype(F32)
    left = jnp.concatenate([normed[:, 0:HALF], table], axis=1)
    right = jnp.concatenate([normed[:, HALF:D], jnp.zeros((ROW, LANES), F32)], axis=1)
    pay[...] = jnp.concatenate([left, right], axis=0).astype(BF16)


def kernel(
    q, nk, nv, ck, cv, lengths, res, gain, router, gate, up, down, slot_rows, slot_count,
    out,
    kbuf, vbuf, stream, pay, arrived, back, fold,
    rows, parts, t1, t2, t3, t4, wide, wdown, hidden,
    kv_sems, w_sems, pay_send, pay_recv, g_send, g_recv, x_send, x_recv, p_send, p_recv, r_send, r_recv,
    b_send, b_recv,
):
    side, me = lax.axis_index("side"), lax.axis_index("dev")
    z, x, y = me // 16, lax.rem(me // 4, 4), lax.rem(me, 4)
    xp, x2, xm = (lax.rem(x + k, 4) for k in (1, 2, 3))
    yp, y2, ym = (lax.rem(y + k, 4) for k in (1, 2, 3))

    def at(z, x, y):
        return z * 16 + x * 4 + y

    near, far = at(1 - z, x, y), me
    barrier = pltpu.get_barrier_semaphore()

    def greet(side, dev):
        pl.semaphore_signal(barrier, inc=1, device_id={"side": side, "dev": dev}, device_id_type=MESH)

    def remote(src, dst, send, recv, side, dev):
        return pltpu.make_async_remote_copy(
            src_ref=src, dst_ref=dst, send_sem=send, recv_sem=recv,
            device_id={"side": side, "dev": dev}, device_id_type=MESH,
        )

    is_far_pod, is_hub, is_expert = side < 2, side == 2, side == 3

    @pl.when(is_far_pod)
    def _():
        greet(2, near)
        greet(2, far)

    @pl.when(is_hub)
    def _():
        for dev in (at(z, xp, y), at(z, xm, y), at(z, x, yp), at(z, x, ym), at(1 - z, x, y)):
            greet(2, dev)
        greet(3, me)
        for s in range(2):
            greet(s, near)
            greet(s, far)

    @pl.when(is_expert)
    def _():
        greet(2, me)

    def load_weights():
        copies = []
        for n in range(TILES):
            span = pl.ds(n * LANES, LANES)
            copies.append(
                pltpu.make_async_copy(gate.at[0, :, span], wide.at[n, :, pl.ds(0, LANES)], w_sems.at[0, n])
            )
            copies.append(
                pltpu.make_async_copy(up.at[0, :, span], wide.at[n, :, pl.ds(LANES, LANES)], w_sems.at[1, n])
            )
        copies.append(pltpu.make_async_copy(down.at[0], wdown, w_sems.at[2, 0]))
        return copies

    @pl.when(is_expert)
    def _():
        for copy in load_weights():
            copy.start()

    @pl.when(jnp.logical_not(is_expert))
    def _():
        attention(
            q, nk, nv, ck.at[0, 0], cv.at[0, 0], lengths, res, gain, router, slot_rows, slot_count,
            kbuf, vbuf, stream, pay, kv_sems,
        )

    pl.semaphore_wait(barrier, jnp.where(is_hub, 10, jnp.where(is_expert, 1, 2)))

    def unfold(block):
        return block[0:ROW], block[ROW : 2 * ROW]

    def finish():
        left0, right0 = unfold(back[0].astype(F32))
        left1, right1 = unfold(back[1].astype(F32))
        for start, mix in ((0, left0 + left1), (HALF, right0 + right1)):
            mix = mix.astype(BF16).astype(F32)
            out[0, 0, :, start : start + HALF] = (stream[:, start : start + HALF] + mix).astype(BF16)

    @pl.when(is_far_pod)
    def _():
        sent = [
            remote(pay, arrived.at[side], pay_send.at[0], pay_recv.at[side], 2, near),
            remote(pay, arrived.at[2 + side], pay_send.at[1], pay_recv.at[2 + side], 2, far),
        ]
        for copy in sent:
            copy.start()
        for copy in sent:
            copy.wait_send()
        for k in range(2):
            remote(back.at[k], back.at[k], b_send.at[0], b_recv.at[k], 2, me).wait_recv()
        finish()

    @pl.when(is_hub)
    def _():
        right_x, left_x = at(z, xp, y), at(z, xm, y)
        right_y, left_y = at(z, x, yp), at(z, x, ym)
        other = at(1 - z, x, y)
        started = []

        def go(copy):
            copy.start()
            started.append(copy)
            return copy

        trade = go(remote(pay, arrived.at[4], pay_send.at[0], pay_recv.at[4], 2, other))

        def take(slot):
            remote(arrived.at[slot], arrived.at[slot], pay_send.at[1], pay_recv.at[slot], 2, other).wait_recv()

        def pack(c):
            if c == 1:
                trade.wait_recv()
                first, second = pay[...].astype(F32), arrived[4].astype(F32)
            else:
                take(c)
                take(c + 1)
                first, second = arrived[c].astype(F32), arrived[c + 1].astype(F32)
            for begin, row, span in ((0, 0, (0, HALF)), (HALF, ROW, (0, HALF)), (D, 0, (HALF, PAY))):
                block = jnp.concatenate(
                    [first[row : row + ROW, span[0] : span[1]], second[row : row + ROW, span[0] : span[1]]],
                    axis=0,
                )
                rows[c, y, x, :, begin : begin + span[1] - span[0]] = block.astype(BF16)

        def ring(c, half, k, src, dst, dev):
            return go(remote(src, dst, g_send.at[c, half, k], g_recv.at[c, half, k], 2, dev))

        flights = {}

        def push(c, half, k, ref):
            go(remote(ref, ref, x_send.at[c, half, k], x_recv.at[c], 3, me))

        def line(c, half, j):
            begin, stop = (LEFT, RIGHT)[half]
            span = cols(begin, stop)
            return rows.at[c, j, :, :, span] if half == 0 else rows.at[c, :, j, :, span]

        def gather(c, step):
            for half in range(2):
                begin, stop = (LEFT, RIGHT)[half]
                whole, first, second = cols(begin, stop), cols(begin, begin + QUARTER), cols(begin + QUARTER, stop)
                along, across = ((x, xp, xm), (y, yp, ym))[:: 1 if half == 0 else -1]
                to_p, to_m = ((right_x, left_x), (right_y, left_y))[half]
                on_p, on_m = ((right_y, left_y), (right_x, left_x))[half]

                def slot(j, span):
                    return rows.at[c, y, j, :, span] if half == 0 else rows.at[c, j, x, :, span]

                def band(j, span):
                    return rows.at[c, j, :, :, span] if half == 0 else rows.at[c, :, j, :, span]

                key = (c, half)
                if step > 1:
                    for copy in flights[key]:
                        copy.wait_recv()
                if step == 1:
                    src = slot(along[0], whole)
                    flights[key] = [ring(c, half, 0, src, src, to_p), ring(c, half, 1, src, src, to_m)]
                elif step == 2:
                    a, b = slot(along[2], first), slot(along[1], second)
                    flights[key] = [ring(c, half, 2, a, a, to_p), ring(c, half, 3, b, b, to_m)]
                elif step == 3:
                    src = band(across[0], whole)
                    flights[key] = [ring(c, half, 4, src, src, on_p), ring(c, half, 5, src, src, on_m)]
                    push(c, half, 0, src)
                elif step == 4:
                    a, b = band(across[2], first), band(across[1], second)
                    flights[key] = [ring(c, half, 6, a, a, on_p), ring(c, half, 7, b, b, on_m)]
                    push(c, half, 1, band(across[1], whole))
                    push(c, half, 2, band(across[2], whole))
                else:
                    push(c, half, 3, band((y2, x2)[half], whole))

        sums = {}

        def leg(c, half, k, src, dst, dev):
            return go(remote(src, dst, r_send.at[c, half, k], r_recv.at[c, half, k], 2, dev))

        def reduce(c, step):
            for half in range(2):
                begin = half * HALF
                q0, q1 = (begin, begin + QUARTER), (begin + QUARTER, begin + HALF)
                whole = (begin, begin + HALF)
                across, along = ((y, yp, y2, ym), (x, xp, x2, xm))[:: 1 if half == 0 else -1]
                on_p, on_m = ((right_y, left_y), (right_x, left_x))[half]
                to_p, to_m = ((right_x, left_x), (right_y, left_y))[half]

                def slot(j, span):
                    span = cols(*span)
                    return parts.at[c, y, j, :, span] if half == 0 else parts.at[c, j, x, :, span]

                def band(j, span):
                    span = cols(*span)
                    return parts.at[c, j, :, :, span] if half == 0 else parts.at[c, :, j, :, span]

                def cell(j, i, span):
                    span = cols(*span)
                    return parts.at[c, j, i, :, span] if half == 0 else parts.at[c, i, j, :, span]

                key = (c, half)
                b1, b2, b3, b4 = t1.at[c, half], t2.at[c, half], t3.at[c, half], t4.at[c, half]
                if step == 1:
                    for quarter, span in enumerate((q0, q1)):
                        ref = parts.at[c, :, :, :, cols(*span)]
                        k = 2 * half + quarter
                        remote(ref, ref, p_send.at[c, k], p_recv.at[c, k], 3, me).wait_recv()
                    sums[key] = [
                        leg(c, half, 0, band(across[2], q0), b1.at[0], on_p),
                        leg(c, half, 1, band(across[2], q1), b1.at[1], on_m),
                    ]
                elif step == 2:
                    flying = []
                    for k, (j, span, dev) in enumerate(((across[1], q0, on_p), (across[3], q1, on_m))):
                        sums[key][k].wait_recv()
                        for i in range(4):
                            ref = cell(j, i, span)
                            ref[...] = (ref[...].astype(F32) + b1[k, i].astype(F32)).astype(BF16)
                        flying.append(leg(c, half, 2 + k, band(j, whole), b2.at[k], dev))
                    sums[key] = flying
                elif step == 3:
                    for copy in sums[key]:
                        copy.wait_recv()
                    for i in range(4):
                        ref = cell(across[0], i, whole)
                        ref[...] = (ref[...].astype(F32) + b2[0, i].astype(F32) + b2[1, i].astype(F32)).astype(BF16)
                    sums[key] = [
                        leg(c, half, 4, slot(along[2], q0), b3.at[0], to_p),
                        leg(c, half, 5, slot(along[2], q1), b3.at[1], to_m),
                    ]
                elif step == 4:
                    flying = []
                    for k, (j, span, dev) in enumerate(((along[1], q0, to_p), (along[3], q1, to_m))):
                        sums[key][k].wait_recv()
                        ref = slot(j, span)
                        ref[...] = (ref[...].astype(F32) + b3[k].astype(F32)).astype(BF16)
                        flying.append(leg(c, half, 6 + k, slot(j, whole), b4.at[k], dev))
                    sums[key] = flying
                else:
                    for copy in sums[key]:
                        copy.wait_recv()
                    ref = slot(along[0], whole)
                    block = ref[...].astype(F32) + b4[0].astype(F32) + b4[1].astype(F32)
                    sums[key] = block
            if step == 5:
                left, right = sums[(c, 0)], sums[(c, 1)]
                folded = [
                    jnp.concatenate([left[s * ROW : (s + 1) * ROW], right[s * ROW : (s + 1) * ROW]], axis=0)
                    for s in range(2)
                ]
                if c == 1:
                    back[0] = folded[0].astype(BF16)
                    fold[c, 1] = folded[1].astype(BF16)
                    sums["own"] = go(remote(fold.at[c, 1], back.at[1], b_send.at[c, 1], b_recv.at[1], 2, other))
                else:
                    for s in range(2):
                        fold[c, s] = folded[s].astype(BF16)
                        dev, k = (near, 0) if c == 0 else (far, 1)
                        go(remote(fold.at[c, s], back.at[k], b_send.at[c, s], b_recv.at[k], s, dev))

        pack(0)
        gather(0, 1)
        pack(1)
        gather(0, 2)
        gather(1, 1)
        pack(2)
        gather(0, 3)
        gather(1, 2)
        gather(2, 1)
        gather(0, 4)
        gather(1, 3)
        gather(2, 2)
        gather(0, 5)
        gather(1, 4)
        gather(2, 3)
        gather(1, 5)
        gather(2, 4)
        gather(2, 5)
        for c in range(CHUNKS):
            for step in range(1, 6):
                reduce(c, step)
        sums["own"].wait_recv()
        finish()
        for copy in started:
            copy.wait_send()

    @pl.when(is_expert)
    def _():
        expert = me // 8
        for copy in load_weights():
            copy.wait()
        lane = lax.broadcasted_iota(jnp.int32, (2 * LANES, LANES), 1)
        mine = (lane == expert) | (lane == expert + EXP)

        def send(c, k):
            ref = parts.at[c, :, :, :, pl.ds(k * QUARTER, QUARTER)]
            return remote(ref, ref, p_send.at[c, k], p_recv.at[c, k], 2, me)

        for c in range(CHUNKS):
            remote(rows.at[c], rows.at[c], x_send.at[c, 0, 0], x_recv.at[c], 2, me).wait_recv()
            table = rows[c, :, :, :, D:WIDE].reshape(2 * LANES, LANES).astype(F32)
            weight = jnp.sum(jnp.where(mine, table, 0.0), axis=1, keepdims=True)

            def units(n, carry):
                block = rows[c, :, :, :, 0:D].reshape(2 * LANES, D)
                both = jnp.dot(block, wide[n], preferred_element_type=F32)
                g, u = both[:, 0:LANES], both[:, LANES:]
                value = g * u / (1.0 + jnp.exp(-g)) * weight
                hidden[:, pl.ds(pl.multiple_of(n * LANES, LANES), LANES)] = value.astype(BF16)
                return carry

            lax.fori_loop(0, TILES, units, 0)
            for k in range(4):
                span = slice(k * QUARTER, (k + 1) * QUARTER)
                made = jnp.dot(hidden[...], wdown[:, span], preferred_element_type=F32)
                parts[c, :, :, :, span] = made.astype(BF16).reshape(4, 4, 2 * ROW, QUARTER)
                send(c, k).start()
        out[...] = jnp.zeros_like(out)
        for c in range(CHUNKS):
            for k in range(4):
                send(c, k).wait_send()


def local(
    query, new_key, new_value, cache_key, cache_value, lengths, residual,
    norm_gain, router_weight, gate_weight, up_weight, down_weight, slot_rows, slot_count,
):
    vmem, smem, hbm = (
        pl.BlockSpec(memory_space=pltpu.VMEM),
        pl.BlockSpec(memory_space=pltpu.SMEM),
        pl.BlockSpec(memory_space=pl.ANY),
    )
    dma = pltpu.SemaphoreType.DMA
    return pl.pallas_call(
        kernel,
        out_shape=jax.ShapeDtypeStruct(query.shape, BF16),
        in_specs=[vmem, vmem, vmem, hbm, hbm, smem, vmem, vmem, vmem, hbm, hbm, hbm, smem, smem],
        out_specs=vmem,
        scratch_shapes=[
            pltpu.VMEM((ROW, CTX, KVH * HD), BF16),
            pltpu.VMEM((ROW, CTX, KVH * HD), BF16),
            pltpu.VMEM((ROW, D), F32),
            pltpu.VMEM((2 * ROW, PAY), BF16),
            pltpu.VMEM((5, 2 * ROW, PAY), BF16),
            pltpu.VMEM((2, 2 * ROW, HALF), BF16),
            pltpu.VMEM((CHUNKS, 2, 2 * ROW, HALF), BF16),
            pltpu.VMEM((CHUNKS, 4, 4, 2 * ROW, WIDE), BF16),
            pltpu.VMEM((CHUNKS, 4, 4, 2 * ROW, D), BF16),
            pltpu.VMEM((CHUNKS, 2, 2, 4, 2 * ROW, QUARTER), BF16),
            pltpu.VMEM((CHUNKS, 2, 2, 4, 2 * ROW, HALF), BF16),
            pltpu.VMEM((CHUNKS, 2, 2, 2 * ROW, QUARTER), BF16),
            pltpu.VMEM((CHUNKS, 2, 2, 2 * ROW, HALF), BF16),
            pltpu.VMEM((TILES, D, 2 * LANES), BF16),
            pltpu.VMEM((UNITS, D), BF16),
            pltpu.VMEM((2 * LANES, UNITS), BF16),
            dma((2, 4)),
            dma((3, TILES)),
            dma((2,)),
            dma((5,)),
            dma((CHUNKS, 2, 8)),
            dma((CHUNKS, 2, 8)),
            dma((CHUNKS, 2, 4)),
            dma((CHUNKS,)),
            dma((CHUNKS, 4)),
            dma((CHUNKS, 4)),
            dma((CHUNKS, 2, 8)),
            dma((CHUNKS, 2, 8)),
            dma((CHUNKS, 2)),
            dma((2,)),
        ],
        compiler_params=pltpu.CompilerParams(
            collective_id=0, has_side_effects=True, vmem_limit_bytes=56 * 2**20
        ),
        name="moe_block",
    )(
        query, new_key, new_value, cache_key, cache_value, lengths, residual,
        norm_gain.reshape(1, D), jnp.transpose(router_weight),
        gate_weight, up_weight, down_weight, slot_rows, slot_count,
    )


def solution(mesh):
    return jax.shard_map(
        local,
        mesh=mesh,
        in_specs=(
            P("side", "dev", None, None),
            P("side", "dev", None, None),
            P("side", "dev", None, None),
            P("side", "dev", None, None, None),
            P("side", "dev", None, None, None),
            P("side", "dev", None),
            P("side", "dev", None, None),
            P(),
            P(),
            P("side", None, "dev"),
            P("side", None, "dev"),
            P("side", "dev", None),
            P("side", "dev", None, None),
            P("side", "dev", None),
        ),
        out_specs=P("side", "dev", None, None),
        check_vma=False,
    )
```

time: 284 us -> 113 us (0.40)
  waiting for transfers between devices: 157 us -> 0 us
  Pallas kernels: 0 us -> 112 us
  blocking collectives: 82.1 us -> 0 us
  between operations: 13.6 us -> 0.01 us
  local copies, waits for them, and re-layouts: 11.9 us -> 1.47 us
  matrix products: 7.09 us -> 0 us
  starting transfers between devices: 7.06 us -> 0 us
  other arithmetic: 4.85 us -> 0 us
    pallas_call x0 -> x1, Pallas kernels: none -> 112 us  [local(): pl.pallas_call(kernel, out_shape=jax.ShapeDtypeStruct(query.shape, BF16),...]
    all_to_all x1 -> x0, waiting for transfers between devices: 86.6 us -> none  [local(): lax.all_to_all(sectioned, 'dev', split_axis=0, concat_axis=0, tiled=True)]
    all_to_all x1 -> x0, blocking collectives: 82.1 us -> none  [local(): lax.all_to_all(partial_value.astype(jnp.bfloat16), 'dev', split_axis=0, c...]
    psum x1 -> x0, waiting for transfers between devices: 45.6 us -> none  [spread(): return lax.psum(kept, axis)]
    all_gather x1 -> x0, waiting for transfers between devices: 24.7 us -> none  [local(): lax.all_gather(outgoing[:, None], 'side', axis=1, tiled=True)[:, :pod_count]]
    dot_general x6 -> x0, matrix products: 7.09 us -> none  [the longest x1 2.11 us: attend(): jnp.einsum('rkgd,rckd->rkgc', queries, keys_all, preferred_element_type=j...]
    all_to_all x1 -> x0, starting transfers between devices: 7.02 us -> none  [local(): lax.all_to_all(sectioned, 'dev', split_axis=0, concat_axis=0, tiled=True)]
    broadcast_in_dim x1 -> x0, local copies, waits for them, and re-layouts: 3.44 us -> none  [local(): jnp.broadcast_to(arrived[:, None], (expert_count, shard_count) + arrived....]
  transfers between devices with their start and end apart: 3 -> 0, of which waited for: 3 -> 0; matrix products, arithmetic and copies ran while one was open for 0% -> 0% of each run, Pallas kernels for 0% -> 0%
where the time goes in v1:
time: 113 us
  Pallas kernels  112 us (99%)
  local copies, waits for them, and re-layouts  1.47 us (1%)
    pallas_call x1, Pallas kernels, local(): pl.pallas_call(kernel, out_shape=jax.ShapeDtypeStruct(query.shape, BF16),...  112 us

profile of v1, /device:TPU:1, one launch (start us, length us, event | category | flops | bytes accessed | tf_op | source)
XLA Modules:
  0.0 113.2 jit_solution(4280825236139589893)
XLA Ops:
  0.0 111.7 %moe_block.1 = bf16[1,1,8,4096]{3,2,1,0:T(8,128)(2,1)} custom-call(bf16[1,1,8,4096]{3,2,1,0:T(8,128)(2,1)} %q.1, bf16[1,1,8,1024]{3,2,1,0:T(8,128)(2,1)} %nk.1, bf16[1,1,8,1024]{3,2,1,0:T(8,128)(2,1)} %nv.1, bf16[1,1,8,128,1024]{4,3,2,1,0:T(8,128)(2,1)} %ck.1, bf16[1,1,8,128,1024]{4,3,2,1,0:T(8,128)(2,1)} %cv.1, s32[1,1,8]{2,1,0:T(1,128)} %lengths.1, ...), custom_call_target="tpu_custom_call" | custom-call | tf_op jit(solution)/shard_map/moe_block/pallas_call | solution.py:445
  111.7 1.5 %copy.16 = bf16[1,1,8,4096]{3,2,1,0:T(8,128)(2,1)} copy(bf16[1,1,8,4096]{3,2,1,0:T(8,128)(2,1)} %moe_block.1) | data formatting | bytes 131072

commit v2 on v1

v2 whole, which is shorter than its diff:
```python
import functools
import math

import jax
import jax.numpy as jnp
from jax import lax
from jax.experimental import pallas as pl
from jax.experimental.pallas import tpu as pltpu
from jax.sharding import PartitionSpec as P

MESH = pl.DeviceIdType.MESH
F32 = jnp.float32
BF16 = jnp.bfloat16

HD = 128
KVH = 8
GROUP = 4
EXP = 4
ROW = 8
CTX = 128
D = 4096
HALF = D // 2
QUARTER = D // 4
LANES = 128
WIDE = D + LANES
PAY = HALF + LANES
UNITS = 896
TILES = UNITS // LANES
CHUNKS = 3
LEFT, RIGHT = (0, HALF), (HALF, WIDE)
NEG = -1e30
ORDER = (0, 2, 1, 3)


def cols(start, stop):
    return pl.ds(start, stop - start)


def attention(q, nk, nv, ck, cv, lengths, res, gain, router, slot_rows, slot_count, kbuf, vbuf, stream, pay, sems):
    pieces = 4
    wide = KVH * HD // pieces

    def load(source, target, which, piece):
        span = pl.ds(piece * wide, wide)
        return pltpu.make_async_copy(source.at[:, :, span], target.at[:, :, span], sems.at[which, piece])

    for piece in range(pieces):
        load(ck, kbuf, 0, piece).start()
        load(cv, vbuf, 1, piece).start()
    scale = 1.0 / math.sqrt(HD)
    sub = lax.broadcasted_iota(jnp.int32, (ROW, LANES), 0)
    lane = lax.broadcasted_iota(jnp.int32, (ROW, LANES), 1)
    bias = jnp.concatenate(
        [jnp.where((sub == r) & (lane < lengths[0, 0, r]), 0.0, NEG) for r in range(ROW)], axis=1
    ).astype(F32)
    bias = jnp.concatenate([bias] * GROUP, axis=0)
    total = jnp.zeros((ROW, 1), F32)
    for k in range(KVH):
        if k % (KVH // pieces) == 0:
            load(ck, kbuf, 0, k // (KVH // pieces)).wait()
            load(cv, vbuf, 1, k // (KVH // pieces)).wait()
        span = slice(k * HD, (k + 1) * HD)
        heads = [slice((k * GROUP + g) * HD, (k * GROUP + g + 1) * HD) for g in range(GROUP)]
        query = jnp.concatenate([q[0, 0, :, h].astype(F32) for h in heads], axis=0)
        new_key = jnp.concatenate([nk[0, 0, :, span].astype(F32)] * GROUP, axis=0)
        new_value = jnp.concatenate([nv[0, 0, :, span].astype(F32)] * GROUP, axis=0)
        keys = kbuf[:, :, span].reshape(ROW * CTX, HD)
        values = vbuf[:, :, span].reshape(ROW * CTX, HD)
        scores = lax.dot_general(
            query.astype(BF16), keys, (((1,), (1,)), ((), ())), preferred_element_type=F32
        )
        scores = scores * scale + bias
        own = jnp.sum(query * new_key, axis=1, keepdims=True) * scale
        top = jnp.maximum(jnp.max(scores, axis=1, keepdims=True), own)
        probs = jnp.exp(scores - top)
        own_prob = jnp.exp(own - top)
        inverse = 1.0 / (jnp.sum(probs, axis=1, keepdims=True) + own_prob)
        weights = (probs * inverse).astype(BF16)
        own_weight = (own_prob * inverse).astype(BF16).astype(F32)
        context = jnp.dot(weights, values, preferred_element_type=F32) + own_weight * new_value
        for g, h in enumerate(heads):
            part = res[0, 0, :, h].astype(F32) + context[g * ROW : (g + 1) * ROW]
            stream[:, h] = part
            total = total + jnp.sum(part * part, axis=1, keepdims=True)
    rows = stream[...]
    normed = (rows * lax.rsqrt(total / D + 1e-05) * gain[...]).astype(BF16)
    logits = lax.dot_general(normed, router[...], (((1,), (1,)), ((), ())), preferred_element_type=F32)
    raised = []
    for e in range(EXP):
        chosen = jnp.zeros((ROW, 1), F32)
        for c in range(slot_rows.shape[3]):
            hit = (sub[:, 0:1] == slot_rows[0, 0, e, c]) & (c < slot_count[0, 0, e])
            chosen = chosen + jnp.where(hit, 1.0, 0.0)
        raised.append(chosen * jnp.exp(logits[:, e : e + 1]))
    inverse = raised[0] + raised[1] + raised[2] + raised[3]
    table = jnp.zeros((ROW, LANES), F32)
    for e in range(EXP):
        weight = raised[e] / inverse
        high = weight.astype(BF16).astype(F32)
        table = table + jnp.where(lane == e, high, 0.0) + jnp.where(lane == EXP + e, weight - high, 0.0)
    normed = normed.astype(F32)
    left = jnp.concatenate([normed[:, 0:HALF], table], axis=1)
    right = jnp.concatenate([normed[:, HALF:D], jnp.zeros((ROW, LANES), F32)], axis=1)
    pay[...] = jnp.concatenate([left, right], axis=0).astype(BF16)


def kernel(
    q, nk, nv, ck, cv, lengths, res, gain, router, gate, up, down, slot_rows, slot_count,
    out,
    kbuf, vbuf, stream, pay, arrived, back, fold,
    rows, parts, landed, merged, crossed, wide, wdown, hidden,
    kv_sems, w_sems, pay_send, pay_recv, g_send, g_recv, p_send, p_recv, r_send, r_recv, b_send, b_recv,
):
    side, me = lax.axis_index("side"), lax.axis_index("dev")
    z, x, y = me // 16, lax.rem(me // 4, 4), lax.rem(me, 4)
    xs = [x] + [lax.rem(x + k, 4) for k in (1, 2, 3)]
    ys = [y] + [lax.rem(y + k, 4) for k in (1, 2, 3)]

    def at(z, x, y):
        return z * 16 + x * 4 + y

    near, far = at(1 - z, x, y), me
    in_line = [at(z, xs[k], y) for k in (1, 2, 3)] + [at(z, x, ys[k]) for k in (1, 2, 3)]
    barrier = pltpu.get_barrier_semaphore()

    def greet(side, dev):
        pl.semaphore_signal(barrier, inc=1, device_id={"side": side, "dev": dev}, device_id_type=MESH)

    def remote(src, dst, send, recv, side, dev):
        return pltpu.make_async_remote_copy(
            src_ref=src, dst_ref=dst, send_sem=send, recv_sem=recv,
            device_id={"side": side, "dev": dev}, device_id_type=MESH,
        )

    is_far_pod, is_hub, is_expert = side < 2, side == 2, side == 3

    @pl.when(is_far_pod)
    def _():
        for s in (2, 3):
            greet(s, near)
            greet(s, far)

    @pl.when(jnp.logical_not(is_far_pod))
    def _():
        for s in (2, 3):
            for dev in in_line:
                greet(s, dev)
        greet(5 - side, me)
        greet(5 - side, near)
        for s in (0, 1):
            greet(s, near)
            greet(s, far)

    @pl.when(is_hub)
    def _():
        greet(2, near)

    def load_weights():
        copies = []
        for n in range(TILES):
            span = pl.ds(n * LANES, LANES)
            copies.append(
                pltpu.make_async_copy(gate.at[0, :, span], wide.at[n, :, pl.ds(0, LANES)], w_sems.at[0, n])
            )
            copies.append(
                pltpu.make_async_copy(up.at[0, :, span], wide.at[n, :, pl.ds(LANES, LANES)], w_sems.at[1, n])
            )
        copies.append(pltpu.make_async_copy(down.at[0], wdown, w_sems.at[2, 0]))
        return copies

    @pl.when(is_expert)
    def _():
        for copy in load_weights():
            copy.start()

    @pl.when(jnp.logical_not(is_expert))
    def _():
        attention(
            q, nk, nv, ck.at[0, 0], cv.at[0, 0], lengths, res, gain, router, slot_rows, slot_count,
            kbuf, vbuf, stream, pay, kv_sems,
        )

    pl.semaphore_wait(barrier, jnp.where(is_hub, 19, jnp.where(is_expert, 18, 4)))

    def unfold(block):
        return block[0:ROW], block[ROW : 2 * ROW]

    def finish():
        left0, right0 = unfold(back[0].astype(F32))
        left1, right1 = unfold(back[1].astype(F32))
        for start, mix in ((0, left0 + left1), (HALF, right0 + right1)):
            mix = mix.astype(BF16).astype(F32)
            out[0, 0, :, start : start + HALF] = (stream[:, start : start + HALF] + mix).astype(BF16)

    @pl.when(is_far_pod)
    def _():
        sent = [
            remote(pay, arrived.at[side], pay_send.at[0], pay_recv.at[side], 3, near),
            remote(pay, arrived.at[2 + side], pay_send.at[1], pay_recv.at[2 + side], 3, far),
        ]
        for copy in sent:
            copy.start()
        for copy in sent:
            copy.wait_send()
        for k in range(2):
            remote(back.at[k], back.at[k], b_send.at[0, 0], b_recv.at[k], 2, me).wait_recv()
        finish()

    @pl.when(is_hub)
    def _():
        started = []

        def go(copy):
            copy.start()
            started.append(copy)
            return copy

        go(remote(pay, arrived.at[4], pay_send.at[0], pay_recv.at[4], 3, me))
        go(remote(pay, arrived.at[5], pay_send.at[1], pay_recv.at[5], 3, near))
        flights = {}

        def first(c, u):
            for k in range(4):
                ref = landed.at[c, u, k]
                remote(ref, ref, p_send.at[c, u, k], p_recv.at[c, u, k], 3, me).wait_recv()
            for i in range(4):
                total = landed[c, u, 0, i].astype(F32)
                for k in range(1, 4):
                    total = total + landed[c, u, k, i].astype(F32)
                merged[c, u, i] = total.astype(BF16)
            flights[c, u] = []
            for k in range(1, 4):
                j, dev = (xs[k], at(z, xs[k], y)) if u < 2 else (ys[k], at(z, x, ys[k]))
                flights[c, u].append(
                    go(remote(merged.at[c, u, j], crossed.at[c, u, k - 1], r_send.at[c, u, k - 1], r_recv.at[c, u, k - 1], 2, dev))
                )

        def second(c, u):
            for copy in flights[c, u]:
                copy.wait_recv()
            total = merged[c, u, x if u < 2 else y].astype(F32)
            for k in range(3):
                total = total + crossed[c, u, k].astype(F32)
            return total

        def give(c, sums):
            halves = [jnp.concatenate(sums[0:2], axis=1), jnp.concatenate(sums[2:4], axis=1)]
            folded = [
                jnp.concatenate([half[s * ROW : (s + 1) * ROW] for half in halves], axis=0).astype(BF16)
                for s in range(2)
            ]
            if c == 0:
                back[0] = folded[0]
                fold[c, 1] = folded[1]
                flights["own"] = go(remote(fold.at[c, 1], back.at[1], b_send.at[c, 1], b_recv.at[1], 2, near))
            else:
                for s in range(2):
                    fold[c, s] = folded[s]
                    dev, k = (far, 1) if c == 1 else (near, 0)
                    go(remote(fold.at[c, s], back.at[k], b_send.at[c, s], b_recv.at[k], s, dev))

        for c in range(CHUNKS):
            for u in ORDER:
                first(c, u)
            sums = [second(c, u) for u in range(4)]
            give(c, sums)
        flights["own"].wait_recv()
        finish()
        for copy in started:
            copy.wait_send()

    @pl.when(is_expert)
    def _():
        expert = me // 8
        started = []

        def go(copy):
            copy.start()
            started.append(copy)
            return copy

        def pack(c):
            slots = ((4, 5), (2, 3), (0, 1))[c]
            for slot in slots:
                remote(arrived.at[slot], arrived.at[slot], pay_send.at[0], pay_recv.at[slot], 2, me).wait_recv()
            a, b = (arrived[slot].astype(F32) for slot in slots)
            for begin, row, span in ((0, 0, (0, HALF)), (HALF, ROW, (0, HALF)), (D, 0, (HALF, PAY))):
                block = jnp.concatenate(
                    [a[row : row + ROW, span[0] : span[1]], b[row : row + ROW, span[0] : span[1]]], axis=0
                )
                rows[c, y, x, :, begin : begin + span[1] - span[0]] = block.astype(BF16)

        flights = {}

        def spread(c, phase):
            made = []
            for half in range(2):
                span = cols(*(LEFT, RIGHT)[half])
                for k in (1, 2, 3):
                    on_x = at(z, xs[k], y)
                    on_y = at(z, x, ys[k])
                    if phase == 0:
                        ref, dev = rows.at[c, y, x, :, span], (on_x, on_y)[half]
                    elif half == 0:
                        ref, dev = rows.at[c, y, :, :, span], on_y
                    else:
                        ref, dev = rows.at[c, :, x, :, span], on_x
                    made.append(
                        go(remote(ref, ref, g_send.at[c, phase, half, k - 1], g_recv.at[c, phase, half, k - 1], 3, dev))
                    )
            flights[c, phase] = made

        def gathered(c, phase):
            for copy in flights[c, phase]:
                copy.wait_recv()

        pack(0)
        spread(0, 0)
        pack(2)
        spread(2, 0)
        pack(1)
        spread(1, 0)
        for c in range(CHUNKS):
            gathered(c, 0)
            spread(c, 1)
        for copy in load_weights():
            copy.wait()
        lane = lax.broadcasted_iota(jnp.int32, (2 * LANES, LANES), 1)
        mine = (lane == expert) | (lane == expert + EXP)
        for c in range(CHUNKS):
            gathered(c, 1)
            table = rows[c, :, :, :, D:WIDE].reshape(2 * LANES, LANES).astype(F32)
            weight = jnp.sum(jnp.where(mine, table, 0.0), axis=1, keepdims=True)

            def units(n, carry):
                block = rows[c, :, :, :, 0:D].reshape(2 * LANES, D)
                both = jnp.dot(block, wide[n], preferred_element_type=F32)
                g, u = both[:, 0:LANES], both[:, LANES:]
                value = g * u / (1.0 + jnp.exp(-g)) * weight
                hidden[:, pl.ds(pl.multiple_of(n * LANES, LANES), LANES)] = value.astype(BF16)
                return carry

            lax.fori_loop(0, TILES, units, 0)
            for u in ORDER:
                span = slice(u * QUARTER, (u + 1) * QUARTER)
                made = jnp.dot(hidden[...], wdown[:, span], preferred_element_type=F32)
                parts[c, :, :, :, span] = made.astype(BF16).reshape(4, 4, 2 * ROW, QUARTER)
                for k in range(4):
                    if u < 2:
                        src, dev = parts.at[c, ys[k], :, :, cols(u * QUARTER, (u + 1) * QUARTER)], at(z, x, ys[k])
                    else:
                        src, dev = parts.at[c, :, xs[k], :, cols(u * QUARTER, (u + 1) * QUARTER)], at(z, xs[k], y)
                    go(remote(src, landed.at[c, u, k], p_send.at[c, u, k], p_recv.at[c, u, k], 2, dev))
        out[...] = jnp.zeros_like(out)
        for copy in started:
            copy.wait_send()


def local(
    query, new_key, new_value, cache_key, cache_value, lengths, residual,
    norm_gain, router_weight, gate_weight, up_weight, down_weight, slot_rows, slot_count,
):
    vmem, smem, hbm = (
        pl.BlockSpec(memory_space=pltpu.VMEM),
        pl.BlockSpec(memory_space=pltpu.SMEM),
        pl.BlockSpec(memory_space=pl.ANY),
    )
    dma = pltpu.SemaphoreType.DMA
    return pl.pallas_call(
        kernel,
        out_shape=jax.ShapeDtypeStruct(query.shape, BF16),
        in_specs=[vmem, vmem, vmem, hbm, hbm, smem, vmem, vmem, vmem, hbm, hbm, hbm, smem, smem],
        out_specs=vmem,
        scratch_shapes=[
            pltpu.VMEM((ROW, CTX, KVH * HD), BF16),
            pltpu.VMEM((ROW, CTX, KVH * HD), BF16),
            pltpu.VMEM((ROW, D), F32),
            pltpu.VMEM((2 * ROW, PAY), BF16),
            pltpu.VMEM((6, 2 * ROW, PAY), BF16),
            pltpu.VMEM((2, 2 * ROW, HALF), BF16),
            pltpu.VMEM((CHUNKS, 2, 2 * ROW, HALF), BF16),
            pltpu.VMEM((CHUNKS, 4, 4, 2 * ROW, WIDE), BF16),
            pltpu.VMEM((CHUNKS, 4, 4, 2 * ROW, D), BF16),
            pltpu.VMEM((CHUNKS, 4, 4, 4, 2 * ROW, QUARTER), BF16),
            pltpu.VMEM((CHUNKS, 4, 4, 2 * ROW, QUARTER), BF16),
            pltpu.VMEM((CHUNKS, 4, 3, 2 * ROW, QUARTER), BF16),
            pltpu.VMEM((TILES, D, 2 * LANES), BF16),
            pltpu.VMEM((UNITS, D), BF16),
            pltpu.VMEM((2 * LANES, UNITS), BF16),
            dma((2, 4)),
            dma((3, TILES)),
            dma((2,)),
            dma((6,)),
            dma((CHUNKS, 2, 2, 3)),
            dma((CHUNKS, 2, 2, 3)),
            dma((CHUNKS, 4, 4)),
            dma((CHUNKS, 4, 4)),
            dma((CHUNKS, 4, 3)),
            dma((CHUNKS, 4, 3)),
            dma((CHUNKS, 2)),
            dma((2,)),
        ],
        compiler_params=pltpu.CompilerParams(
            collective_id=0, has_side_effects=True, vmem_limit_bytes=56 * 2**20
        ),
        name="moe_block",
    )(
        query, new_key, new_value, cache_key, cache_value, lengths, residual,
        norm_gain.reshape(1, D), jnp.transpose(router_weight),
        gate_weight, up_weight, down_weight, slot_rows, slot_count,
    )


def solution(mesh):
    return jax.shard_map(
        local,
        mesh=mesh,
        in_specs=(
            P("side", "dev", None, None),
            P("side", "dev", None, None),
            P("side", "dev", None, None),
            P("side", "dev", None, None, None),
            P("side", "dev", None, None, None),
            P("side", "dev", None),
            P("side", "dev", None, None),
            P(),
            P(),
            P("side", None, "dev"),
            P("side", None, "dev"),
            P("side", "dev", None),
            P("side", "dev", None, None),
            P("side", "dev", None),
        ),
        out_specs=P("side", "dev", None, None),
        check_vma=False,
    )
```

time: 113 us -> 74.1 us (0.66)
  Pallas kernels: 112 us -> 72.4 us
    pallas_call x1, Pallas kernels: 112 us -> 72.4 us  [local(): pl.pallas_call(kernel, out_shape=jax.ShapeDtypeStruct(query.shape, BF16),...]
where the time goes in v2:
time: 74.1 us; the launch traced here: 73.9 us
  Pallas kernels  72.4 us (98%)
  local copies, waits for them, and re-layouts  1.47 us (2%)
    pallas_call x1, Pallas kernels, local(): pl.pallas_call(kernel, out_shape=jax.ShapeDtypeStruct(query.shape, BF16),...  72.4 us

profile of v2, /device:TPU:1, one launch (start us, length us, event | category | flops | bytes accessed | tf_op | source)
XLA Modules:
  0.0 73.9 jit_solution(2066629349175267977)
XLA Ops:
  0.0 72.4 %moe_block.1 = bf16[1,1,8,4096]{3,2,1,0:T(8,128)(2,1)} custom-call(bf16[1,1,8,4096]{3,2,1,0:T(8,128)(2,1)} %q.1, bf16[1,1,8,1024]{3,2,1,0:T(8,128)(2,1)} %nk.1, bf16[1,1,8,1024]{3,2,1,0:T(8,128)(2,1)} %nv.1, bf16[1,1,8,128,1024]{4,3,2,1,0:T(8,128)(2,1)} %ck.1, bf16[1,1,8,128,1024]{4,3,2,1,0:T(8,128)(2,1)} %cv.1, s32[1,1,8]{2,1,0:T(1,128)} %lengths.1, ...), custom_call_target="tpu_custom_call" | custom-call | tf_op jit(solution)/shard_map/moe_block/pallas_call | solution.py:369
  72.4 1.5 %copy.16 = bf16[1,1,8,4096]{3,2,1,0:T(8,128)(2,1)} copy(bf16[1,1,8,4096]{3,2,1,0:T(8,128)(2,1)} %moe_block.1) | data formatting | bytes 131072

commit v3 on v2

v3 whole, which is shorter than its diff:
```python
import functools
import math

import jax
import jax.numpy as jnp
from jax import lax
from jax.experimental import pallas as pl
from jax.experimental.pallas import tpu as pltpu
from jax.sharding import PartitionSpec as P

MESH = pl.DeviceIdType.MESH
F32 = jnp.float32
BF16 = jnp.bfloat16

HD = 128
KVH = 8
GROUP = 4
EXP = 4
ROW = 8
CTX = 128
D = 4096
HALF = D // 2
QUARTER = D // 4
LANES = 128
FOLD = HALF + LANES
UNITS = 896
TILES = UNITS // LANES
CHUNKS = 6
SPANS = ((0, QUARTER), (QUARTER, FOLD))
BATCH = 16 * ROW
FIRST, SECOND, LAST = 0, 1, CHUNKS - 1
DIRECT = 5
NEG = -1e30


def cols(start, stop):
    return pl.ds(start, stop - start)


def attention(q, nk, nv, ck, cv, lengths, res, gain, router, slot_rows, slot_count, kbuf, vbuf, stream, pay, sems):
    pieces = 2
    wide = KVH * HD // pieces

    def load(source, target, which, piece):
        span = pl.ds(piece * wide, wide)
        return pltpu.make_async_copy(source.at[:, :, span], target.at[:, :, span], sems.at[which, piece])

    for piece in range(pieces):
        load(ck, kbuf, 0, piece).start()
        load(cv, vbuf, 1, piece).start()
    scale = 1.0 / math.sqrt(HD)
    sub = lax.broadcasted_iota(jnp.int32, (ROW, LANES), 0)
    lane = lax.broadcasted_iota(jnp.int32, (ROW, LANES), 1)
    length = jnp.zeros((ROW, LANES), jnp.int32)
    for r in range(ROW):
        length = jnp.where(sub == r, lengths[0, 0, r], length)
    seen = jnp.concatenate([lane < length] * GROUP, axis=0)
    row = jnp.concatenate([sub] * GROUP, axis=0)
    spans = [slice(k * HD, (k + 1) * HD) for k in range(KVH)]
    scores, own, new_values = [], [], []
    for k, span in enumerate(spans):
        if k % (KVH // pieces) == 0:
            load(ck, kbuf, 0, k // (KVH // pieces)).wait()
        heads = [slice((k * GROUP + g) * HD, (k * GROUP + g + 1) * HD) for g in range(GROUP)]
        query = jnp.concatenate([q[0, 0, :, h].astype(F32) for h in heads], axis=0)
        new_key = jnp.concatenate([nk[0, 0, :, span].astype(F32)] * GROUP, axis=0)
        new_values.append(jnp.concatenate([nv[0, 0, :, span].astype(F32)] * GROUP, axis=0))
        keys = kbuf[:, :, span].reshape(ROW * CTX, HD)
        every = lax.dot_general(query.astype(BF16), keys, (((1,), (1,)), ((), ())), preferred_element_type=F32)
        kept = every[:, 0:CTX]
        for r in range(1, ROW):
            kept = jnp.where(row == r, every[:, r * CTX : (r + 1) * CTX], kept)
        scores.append(jnp.where(seen, kept * scale, NEG))
        own.append(jnp.sum(query * new_key, axis=1, keepdims=True) * scale)
    weights, own_weights = [], []
    for k in range(KVH):
        top = jnp.maximum(jnp.max(scores[k], axis=1, keepdims=True), own[k])
        probs = jnp.exp(scores[k] - top)
        own_prob = jnp.exp(own[k] - top)
        inverse = 1.0 / (jnp.sum(probs, axis=1, keepdims=True) + own_prob)
        weights.append(probs * inverse)
        own_weights.append((own_prob * inverse).astype(BF16).astype(F32))
    total = jnp.zeros((ROW, LANES), F32)
    for k, span in enumerate(spans):
        if k % (KVH // pieces) == 0:
            load(cv, vbuf, 1, k // (KVH // pieces)).wait()
        values = vbuf[:, :, span].reshape(ROW * CTX, HD)
        spaced = jnp.concatenate([jnp.where(row == r, weights[k], 0.0).astype(BF16) for r in range(ROW)], axis=1)
        context = jnp.dot(spaced, values, preferred_element_type=F32) + own_weights[k] * new_values[k]
        for g in range(GROUP):
            h = slice((k * GROUP + g) * HD, (k * GROUP + g + 1) * HD)
            part = res[0, 0, :, h].astype(F32) + context[g * ROW : (g + 1) * ROW]
            stream[:, h] = part
            total = total + part * part
    total = jnp.sum(total, axis=1, keepdims=True)
    rows = stream[...]
    normed = (rows * lax.rsqrt(total / D + 1e-05) * gain[...]).astype(BF16)
    logits = lax.dot_general(normed, router[...], (((1,), (1,)), ((), ())), preferred_element_type=F32)
    raised = []
    for e in range(EXP):
        chosen = jnp.zeros((ROW, 1), F32)
        for c in range(slot_rows.shape[3]):
            hit = (sub[:, 0:1] == slot_rows[0, 0, e, c]) & (c < slot_count[0, 0, e])
            chosen = chosen + jnp.where(hit, 1.0, 0.0)
        raised.append(chosen * jnp.exp(logits[:, e : e + 1]))
    inverse = raised[0] + raised[1] + raised[2] + raised[3]
    table = jnp.zeros((ROW, LANES), F32)
    for e in range(EXP):
        weight = raised[e] / inverse
        high = weight.astype(BF16).astype(F32)
        table = table + jnp.where(lane == e, high, 0.0) + jnp.where(lane == EXP + e, weight - high, 0.0)
    normed = normed.astype(F32)
    upper = [normed[:, 0:QUARTER], normed[:, HALF : HALF + QUARTER], table]
    lower = [normed[:, QUARTER:HALF], normed[:, HALF + QUARTER : D], jnp.zeros((ROW, LANES), F32)]
    pay[...] = jnp.concatenate([jnp.concatenate(upper, axis=1), jnp.concatenate(lower, axis=1)], axis=0).astype(BF16)


def kernel(
    q, nk, nv, ck, cv, lengths, res, gain, router, gate, up, down, slot_rows, slot_count,
    out,
    kbuf, vbuf, stream, pay, back, done,
    rows, parts, turned, passed, merged, crossed, wide, wdown, block, weight, hidden,
    kv_sems, w_sems, pay_send, pay_recv, g_send, g_recv, p_send, p_recv, own_recv, r_send, r_recv, b_send, b_recv,
):
    side, me = lax.axis_index("side"), lax.axis_index("dev")
    z, x, y = me // 16, lax.rem(me // 4, 4), lax.rem(me, 4)
    xs = [x] + [lax.rem(x + k, 4) for k in (1, 2, 3)]
    ys = [y] + [lax.rem(y + k, 4) for k in (1, 2, 3)]

    def at(z, x, y):
        return z * 16 + x * 4 + y

    near, far = at(1 - z, x, y), me
    in_line = [at(z, xs[k], y) for k in (1, 2, 3)] + [at(z, x, ys[k]) for k in (1, 2, 3)]
    barrier = pltpu.get_barrier_semaphore()

    def greet(side, dev):
        pl.semaphore_signal(barrier, inc=1, device_id={"side": side, "dev": dev}, device_id_type=MESH)

    def remote(src, dst, send, recv, side, dev):
        return pltpu.make_async_remote_copy(
            src_ref=src, dst_ref=dst, send_sem=send, recv_sem=recv,
            device_id={"side": side, "dev": dev}, device_id_type=MESH,
        )

    is_far_pod, is_hub, is_expert = side < 2, side == 2, side == 3

    @pl.when(is_far_pod)
    def _():
        for s in (2, 3):
            greet(s, near)
            greet(s, far)
        for dev in in_line:
            greet(side, dev)

    @pl.when(jnp.logical_not(is_far_pod))
    def _():
        for s in (2, 3):
            for dev in in_line:
                greet(s, dev)
        greet(5 - side, me)
        greet(5 - side, near)
        for s in (0, 1):
            greet(s, near)
            greet(s, far)

    @pl.when(is_hub)
    def _():
        greet(2, near)

    def load_weights():
        for n in range(TILES):
            span = pl.ds(n * LANES, LANES)
            pltpu.make_async_copy(gate.at[0, :, span], wide.at[n, :, pl.ds(0, LANES)], w_sems.at[0]).start()
            pltpu.make_async_copy(up.at[0, :, span], wide.at[n, :, pl.ds(LANES, LANES)], w_sems.at[0]).start()
        pltpu.make_async_copy(down.at[0], wdown, w_sems.at[1]).start()

    @pl.when(is_expert)
    def _():
        load_weights()

    @pl.when(jnp.logical_not(is_expert))
    def _():
        attention(
            q, nk, nv, ck.at[0, 0], cv.at[0, 0], lengths, res, gain, router, slot_rows, slot_count,
            kbuf, vbuf, stream, pay, kv_sems,
        )

    pl.semaphore_wait(barrier, jnp.where(is_hub, 19, jnp.where(is_expert, 18, 10)))

    def finish():
        for h in range(2):
            mix = back[0, h].astype(F32) + back[1, h].astype(F32)
            for k in range(2):
                span = slice((2 * h + k) * QUARTER, (2 * h + k + 1) * QUARTER)
                part = mix[k * ROW : (k + 1) * ROW].astype(BF16).astype(F32)
                out[0, 0, :, span] = (stream[:, span] + part).astype(BF16)

    def arrived(ref, sem):
        remote(ref, ref, pay_send.at[0], sem, side, me).wait_recv()

    def sent(ref, sem):
        remote(ref, ref, sem, pay_recv.at[0], side, me).wait_send()

    def give_rows(c, dev):
        remote(pay, rows.at[c, y, x], pay_send.at[0], pay_recv.at[c], 3, dev).start()

    here = (ys, xs)
    line_devs = ([at(z, x, ys[k]) for k in range(4)], [at(z, xs[k], y) for k in range(4)])

    def band(ref, h, j, span=slice(None)):
        return ref.at[j, :, :, span] if h == 0 else ref.at[:, j, :, span]

    def spread(c, phase, straight):
        for h in range(2):
            begin, stop = SPANS[h]
            whole = cols(begin, stop)
            halves = cols(begin, begin + QUARTER // 2), cols(begin + QUARTER // 2, stop)

            def send(ref, which, dev):
                remote(ref, ref, g_send.at[which], g_recv.at[c, phase], side, dev).start()

            if phase == 0:
                for k in (1, 2, 3):
                    send(rows.at[c, y, x, :, whole], 0, line_devs[1 - h][k])
            elif phase == 1:
                for k in (1, 3, 2) if straight else (1, 3):
                    send(band(rows.at[c], h, here[h][0], whole), 2 if straight else 1, line_devs[h][k])
            else:
                send(band(rows.at[c], h, here[h][3], halves[0]), 1, line_devs[h][1])
                send(band(rows.at[c], h, here[h][1], halves[1]), 1, line_devs[h][3])

    def landed(c, phase, straight):
        ref = rows.at[c, 0, 0:3] if phase == 0 else rows.at[c, 0 : 3 if straight else 3 - phase]
        arrived(ref, g_recv.at[c, phase])

    @pl.when(is_far_pod)
    def _():
        @pl.when(side == 1)
        def _():
            give_rows(LAST - 1, near)
            give_rows(3, far)
            sent(rows.at[0, 0, 0:2], pay_send.at[0])

        @pl.when(side == 0)
        def _():
            rows[LAST, y, x] = pay[...]
            spread(LAST, 0, True)
            give_rows(2, far)
            landed(LAST, 0, True)
            spread(LAST, 1, True)

            def push(k):
                for h in range(2):
                    ref = band(rows.at[LAST], h, here[h][k], cols(*SPANS[h]))
                    remote(ref, ref, p_send.at[0], g_recv.at[LAST, 2], 3, near).start()

            push(0)
            landed(LAST, 1, True)
            for k in (1, 3, 2):
                push(k)
            sent(rows.at[0, 0, 0:1], pay_send.at[0])
            sent(rows.at[LAST, 0, 0:3], g_send.at[0])
            sent(rows.at[LAST, 0:3], g_send.at[2])
            sent(rows.at[LAST], p_send.at[0])

        arrived(back, b_recv.at[0])
        finish()

    @pl.when(is_hub)
    def _():
        give_rows(0, me)
        give_rows(1, near)

        def cell(c, h, j, i):
            return parts.at[c, h, j, i] if h == 0 else parts.at[c, h, i, j]

        def first(c, h):
            arrived(parts.at[c, h], own_recv.at[c, h])
            arrived(turned.at[c, h], p_recv.at[c, h])
            if c == CHUNKS - 1:
                return
            for k, step in enumerate((1, 3)):
                span = slice(k * QUARTER // 2, (k + 1) * QUARTER // 2)
                for i in range(4):
                    ref = cell(c, h, here[h][step], i).at[:, span]
                    ref[...] = (ref[...].astype(F32) + turned[c, h, k, i].astype(F32)).astype(BF16)
                src = band(parts.at[c, h], h, here[h][step])
                remote(src, passed.at[c, h, k], r_send.at[0], r_recv.at[c, h], 2, line_devs[h][step]).start()

        def middle(c, h):
            arrived(passed.at[c, h], r_recv.at[c, h])
            for i in range(4):
                total = cell(c, h, here[h][0], i)[...].astype(F32) + passed[c, h, 0, i].astype(F32)
                total = total + passed[c, h, 1, i].astype(F32)
                if c == CHUNKS - 1:
                    halves = [turned[c, h, k, i].astype(F32) for k in range(2)]
                    total = total + jnp.concatenate(halves, axis=1)
                merged[c, h, i] = total.astype(BF16)
            for k in range(1, 4):
                src, dst = merged.at[c, h, here[1 - h][k]], crossed.at[c, h, k - 1]
                remote(src, dst, r_send.at[1], r_recv.at[c, 2], 2, line_devs[1 - h][k]).start()

        def second(c):
            target = back.at[0] if c == 0 else done.at[c]
            arrived(crossed.at[c], r_recv.at[c, 2])
            for h in range(2):
                total = merged[c, h, here[1 - h][0]].astype(F32)
                for k in range(3):
                    total = total + crossed[c, h, k].astype(F32)
                target[h] = total.astype(BF16)
            if c > 0:
                side, dev, k = ((2, near, 1), (0, far, 1), (1, far, 1), (1, near, 0), (0, near, 0))[c - 1]
                remote(done.at[c], back.at[k], b_send.at[0], b_recv.at[0], side, dev).start()

        def both(step, c):
            for h in range(2):
                step(c, h)

        for c in range(CHUNKS):
            if c < LAST:
                both(first, c)
            if c > 0:
                both(middle, c - 1)
            if c > 1:
                second(c - 2)
        both(first, LAST)
        both(middle, LAST)
        second(LAST - 1)
        second(LAST)
        arrived(back.at[1], b_recv.at[0])
        finish()
        sent(rows.at[0, 0, 0:2], pay_send.at[0])
        sent(passed.at[0 : CHUNKS - 1], r_send.at[0])
        sent(crossed, r_send.at[1])
        sent(done.at[1:CHUNKS], b_send.at[0])

    @pl.when(is_expert)
    def _():
        expert = me // 8

        def is_last(c):
            return isinstance(c, int) and c == LAST

        def widen(c, phase, straight=False):
            landed(c, phase - 1, straight)
            spread(c, phase, straight)

        def share(c, h):
            ref = parts.at[c, h]
            for k, step in enumerate((1, 3)):
                span = pl.ds(k * QUARTER // 2, QUARTER // 2)
                dev = line_devs[h][2 if is_last(c) else step]
                remote(band(ref, h, here[h][2], span), turned.at[c, h, k], p_send.at[0], p_recv.at[c, h], 2, dev).start()
                if is_last(c):
                    src = band(ref, h, here[h][step])
                    remote(src, passed.at[c, h, 1 - k], p_send.at[2], r_recv.at[c, h], 2, line_devs[h][step]).start()
            remote(ref, ref, p_send.at[1], own_recv.at[c, h], 2, me).start()

        for c in range(DIRECT):
            arrived(rows.at[c, y, x], pay_recv.at[c])
            spread(c, 0, False)
        widen(FIRST, 1, True)
        sent(rows.at[FIRST, 0:3], g_send.at[2])
        widen(SECOND, 1, True)
        widen(2, 1)
        pltpu.make_async_copy(wide, wide, w_sems.at[0]).wait()
        pltpu.make_async_copy(wdown, wdown, w_sems.at[1]).wait()
        lane = lax.broadcasted_iota(jnp.int32, (ROW, LANES), 1)
        mine = (lane == expert) | (lane == expert + EXP)

        def unfold(c):
            for i in range(8):
                pair = [rows[c, i // 2, 2 * (i % 2) + k].astype(F32) for k in range(2)]
                to = slice(i * 2 * ROW, (i + 1) * 2 * ROW)
                for k in range(4):
                    row, begin = (k % 2) * ROW, (k // 2) * QUARTER
                    piece = [p[row : row + ROW, begin : begin + QUARTER] for p in pair]
                    block[to, k * QUARTER : (k + 1) * QUARTER] = jnp.concatenate(piece, axis=0).astype(BF16)
                table = [jnp.where(mine, p[0:ROW, HALF:FOLD], 0.0) for p in pair]
                table = [jnp.broadcast_to(jnp.sum(t, axis=1, keepdims=True), (ROW, LANES)) for t in table]
                weight[to, :] = jnp.concatenate(table, axis=0)

        def lift():
            for n in range(TILES):
                both = jnp.dot(block[...], wide[n], preferred_element_type=F32)
                g, u = both[:, 0:LANES], both[:, LANES:]
                hidden[:, n * LANES : (n + 1) * LANES] = (g * u / (1.0 + jnp.exp(-g)) * weight[...]).astype(BF16)

        def lower(c, h):
            made = jnp.dot(hidden[...], wdown[:, h * HALF : (h + 1) * HALF], preferred_element_type=F32)
            made = made.reshape(16, ROW, HALF)
            made = jnp.concatenate([made[:, :, 0:QUARTER], made[:, :, QUARTER:HALF]], axis=1)
            parts[c, h] = made.astype(BF16).reshape(4, 4, 2 * ROW, QUARTER)

        def batch(c, carry):
            lift()

            @pl.when(c + 3 < DIRECT)
            def _():
                widen(jnp.minimum(c + 3, DIRECT - 1), 1)

            lower(c, 0)
            share(c, 0)

            @pl.when(c + 2 < DIRECT)
            def _():
                widen(jnp.minimum(c + 2, DIRECT - 1), 2)

            @pl.when(c + 1 == SECOND)
            def _():
                landed(SECOND, 1, True)

            @pl.when((c + 1 > SECOND) & (c + 1 < DIRECT))
            def _():
                landed(jnp.minimum(c + 1, DIRECT - 1), 2, False)

            @pl.when(c + 1 >= DIRECT)
            def _():
                arrived(rows.at[jnp.maximum(c + 1, DIRECT)], g_recv.at[jnp.maximum(c + 1, DIRECT), 2])

            unfold(c + 1)
            lower(c, 1)
            share(c, 1)
            return carry

        landed(FIRST, 1, True)
        unfold(FIRST)
        lax.fori_loop(0, CHUNKS - 1, batch, 0)
        lift()
        for h in range(2):
            lower(LAST, h)
            share(LAST, h)
        out[...] = jnp.zeros_like(out)
        sent(rows.at[0:DIRECT, 0, 0:3], g_send.at[0])
        sent(rows.at[2:DIRECT, 0:3], g_send.at[1])
        sent(rows.at[SECOND, 0:3], g_send.at[2])
        sent(turned, p_send.at[0])
        sent(parts, p_send.at[1])
        sent(passed.at[LAST], p_send.at[2])


def local(
    query, new_key, new_value, cache_key, cache_value, lengths, residual,
    norm_gain, router_weight, gate_weight, up_weight, down_weight, slot_rows, slot_count,
):
    vmem, smem, hbm = (
        pl.BlockSpec(memory_space=pltpu.VMEM),
        pl.BlockSpec(memory_space=pltpu.SMEM),
        pl.BlockSpec(memory_space=pl.ANY),
    )
    dma = pltpu.SemaphoreType.DMA
    return pl.pallas_call(
        kernel,
        out_shape=jax.ShapeDtypeStruct(query.shape, BF16),
        in_specs=[vmem, vmem, vmem, hbm, hbm, smem, vmem, vmem, vmem, hbm, hbm, hbm, smem, smem],
        out_specs=vmem,
        scratch_shapes=[
            pltpu.VMEM((ROW, CTX, KVH * HD), BF16),
            pltpu.VMEM((ROW, CTX, KVH * HD), BF16),
            pltpu.VMEM((ROW, D), F32),
            pltpu.VMEM((2 * ROW, FOLD), BF16),
            pltpu.VMEM((2, 2, 2 * ROW, QUARTER), BF16),
            pltpu.VMEM((CHUNKS, 2, 2 * ROW, QUARTER), BF16),
            pltpu.VMEM((CHUNKS, 4, 4, 2 * ROW, FOLD), BF16),
            pltpu.VMEM((CHUNKS, 2, 4, 4, 2 * ROW, QUARTER), BF16),
            pltpu.VMEM((CHUNKS, 2, 2, 4, 2 * ROW, QUARTER // 2), BF16),
            pltpu.VMEM((CHUNKS, 2, 2, 4, 2 * ROW, QUARTER), BF16),
            pltpu.VMEM((CHUNKS, 2, 4, 2 * ROW, QUARTER), BF16),
            pltpu.VMEM((CHUNKS, 2, 3, 2 * ROW, QUARTER), BF16),
            pltpu.VMEM((TILES, D, 2 * LANES), BF16),
            pltpu.VMEM((UNITS, D), BF16),
            pltpu.VMEM((BATCH, D), BF16),
            pltpu.VMEM((BATCH, LANES), F32),
            pltpu.VMEM((BATCH, UNITS), BF16),
            dma((2, 2)),
            dma((2,)),
            dma((1,)),
            dma((CHUNKS,)),
            dma((3,)),
            dma((CHUNKS, 3)),
            dma((3,)),
            dma((CHUNKS, 2)),
            dma((CHUNKS, 2)),
            dma((2,)),
            dma((CHUNKS, 3)),
            dma((1,)),
            dma((1,)),
        ],
        compiler_params=pltpu.CompilerParams(
            collective_id=0, has_side_effects=True, vmem_limit_bytes=56 * 2**20
        ),
        name="moe_block",
    )(
        query, new_key, new_value, cache_key, cache_value, lengths, residual,
        norm_gain.reshape(1, D), jnp.transpose(router_weight),
        gate_weight, up_weight, down_weight, slot_rows, slot_count,
    )


def solution(mesh):
    return jax.shard_map(
        local,
        mesh=mesh,
        in_specs=(
            P("side", "dev", None, None),
            P("side", "dev", None, None),
            P("side", "dev", None, None),
            P("side", "dev", None, None, None),
            P("side", "dev", None, None, None),
            P("side", "dev", None),
            P("side", "dev", None, None),
            P(),
            P(),
            P("side", None, "dev"),
            P("side", None, "dev"),
            P("side", "dev", None),
            P("side", "dev", None, None),
            P("side", "dev", None),
        ),
        out_specs=P("side", "dev", None, None),
        check_vma=False,
    )
```

time: 74.1 us -> 67.2 us (0.907)
  the two profiles are of different devices: /device:TPU:1 before, /device:TPU:0 now
where the time goes in v3:
time: 67.2 us; the launch traced here: 67 us
  Pallas kernels  65.5 us (97%)
  local copies, waits for them, and re-layouts  1.47 us (2%)
    pallas_call x1, Pallas kernels, local(): pl.pallas_call(kernel, out_shape=jax.ShapeDtypeStruct(query.shape, BF16),...  65.5 us
    unnamed x1, local copies, waits for them, and re-layouts  1.47 us

profile of v3, /device:TPU:0, one launch (start us, length us, event | category | flops | bytes accessed | tf_op | source)
XLA Modules:
  0.0 67.0 jit_solution(373385539622815135)
XLA Ops:
  0.0 65.5 %moe_block.1 = bf16[1,1,8,4096]{3,2,1,0:T(8,128)(2,1)} custom-call(bf16[1,1,8,4096]{3,2,1,0:T(8,128)(2,1)} %q.1, bf16[1,1,8,1024]{3,2,1,0:T(8,128)(2,1)} %nk.1, bf16[1,1,8,1024]{3,2,1,0:T(8,128)(2,1)} %nv.1, bf16[1,1,8,128,1024]{4,3,2,1,0:T(8,128)(2,1)} %ck.1, bf16[1,1,8,128,1024]{4,3,2,1,0:T(8,128)(2,1)} %cv.1, s32[1,1,8]{2,1,0:T(1,128)} %lengths.1, ...), custom_call_target="tpu_custom_call" | custom-call | tf_op jit(solution)/shard_map/moe_block/pallas_call | solution.py:453
  65.5 1.5 %copy.16 = bf16[1,1,8,4096]{3,2,1,0:T(8,128)(2,1)} copy(bf16[1,1,8,4096]{3,2,1,0:T(8,128)(2,1)} %moe_block.1) | data formatting | bytes 131072

commit v4 on v3

--- a/solution.py
+++ b/solution.py
@@ -28,7 +28,8 @@
 CHUNKS = 6
 SPANS = ((0, QUARTER), (QUARTER, FOLD))
 BATCH = 16 * ROW
-FIRST, SECOND, LAST = 0, 1, CHUNKS - 1
+FIRST, SECOND, LAST, LIFTED = 0, 1, 4, 5
+PASSED = 0
 DIRECT = 5
 NEG = -1e30
 
@@ -238,39 +239,39 @@
     def _():
         @pl.when(side == 1)
         def _():
-            give_rows(LAST - 1, near)
+            give_rows(SECOND, near)
             give_rows(3, far)
             sent(rows.at[0, 0, 0:2], pay_send.at[0])
 
         @pl.when(side == 0)
         def _():
-            rows[LAST, y, x] = pay[...]
-            spread(LAST, 0, True)
+            rows[LIFTED, y, x] = pay[...]
+            spread(LIFTED, 0, True)
             give_rows(2, far)
-            landed(LAST, 0, True)
-            spread(LAST, 1, True)
+            landed(LIFTED, 0, True)
+            spread(LIFTED, 1, True)
 
             def push(k):
                 for h in range(2):
-                    ref = band(rows.at[LAST], h, here[h][k], cols(*SPANS[h]))
-                    remote(ref, ref, p_send.at[0], g_recv.at[LAST, 2], 3, near).start()
+                    ref = band(rows.at[LIFTED], h, here[h][k], cols(*SPANS[h]))
+                    remote(ref, ref, p_send.at[0], g_recv.at[LIFTED, 2], 3, near).start()
 
             push(0)
-            landed(LAST, 1, True)
+            landed(LIFTED, 1, True)
             for k in (1, 3, 2):
                 push(k)
             sent(rows.at[0, 0, 0:1], pay_send.at[0])
-            sent(rows.at[LAST, 0, 0:3], g_send.at[0])
-            sent(rows.at[LAST, 0:3], g_send.at[2])
-            sent(rows.at[LAST], p_send.at[0])
+            sent(rows.at[LIFTED, 0, 0:3], g_send.at[0])
+            sent(rows.at[LIFTED, 0:3], g_send.at[2])
+            sent(rows.at[LIFTED], p_send.at[0])
 
         arrived(back, b_recv.at[0])
         finish()
 
     @pl.when(is_hub)
     def _():
-        give_rows(0, me)
-        give_rows(1, near)
+        give_rows(FIRST, near)
+        give_rows(LAST, me)
 
         def cell(c, h, j, i):
             return parts.at[c, h, j, i] if h == 0 else parts.at[c, h, i, j]
@@ -278,7 +279,7 @@
         def first(c, h):
             arrived(parts.at[c, h], own_recv.at[c, h])
             arrived(turned.at[c, h], p_recv.at[c, h])
-            if c == CHUNKS - 1:
+            if c >= PASSED:
                 return
             for k, step in enumerate((1, 3)):
                 span = slice(k * QUARTER // 2, (k + 1) * QUARTER // 2)
@@ -293,7 +294,7 @@
             for i in range(4):
                 total = cell(c, h, here[h][0], i)[...].astype(F32) + passed[c, h, 0, i].astype(F32)
                 total = total + passed[c, h, 1, i].astype(F32)
-                if c == CHUNKS - 1:
+                if c >= PASSED:
                     halves = [turned[c, h, k, i].astype(F32) for k in range(2)]
                     total = total + jnp.concatenate(halves, axis=1)
                 merged[c, h, i] = total.astype(BF16)
@@ -302,36 +303,40 @@
                 remote(src, dst, r_send.at[1], r_recv.at[c, 2], 2, line_devs[1 - h][k]).start()
 
         def second(c):
-            target = back.at[0] if c == 0 else done.at[c]
+            target = back.at[0] if c == LAST else done.at[c]
             arrived(crossed.at[c], r_recv.at[c, 2])
             for h in range(2):
                 total = merged[c, h, here[1 - h][0]].astype(F32)
                 for k in range(3):
                     total = total + crossed[c, h, k].astype(F32)
                 target[h] = total.astype(BF16)
-            if c > 0:
-                side, dev, k = ((2, near, 1), (0, far, 1), (1, far, 1), (1, near, 0), (0, near, 0))[c - 1]
-                remote(done.at[c], back.at[k], b_send.at[0], b_recv.at[0], side, dev).start()
+            if c != LAST:
+                owners = (2, near, 1), (1, near, 0), (0, far, 1), (1, far, 1), None, (0, near, 0)
+                owner, dev, k = owners[c]
+                remote(done.at[c], back.at[k], b_send.at[0], b_recv.at[0], owner, dev).start()
 
         def both(step, c):
             for h in range(2):
                 step(c, h)
 
-        for c in range(CHUNKS):
-            if c < LAST:
+        order = (0, 1, 2, 3, LIFTED, LAST)
+        for i, c in enumerate(order):
+            if c < PASSED:
                 both(first, c)
-            if c > 0:
-                both(middle, c - 1)
-            if c > 1:
-                second(c - 2)
-        both(first, LAST)
-        both(middle, LAST)
-        second(LAST - 1)
+                if i > 0:
+                    both(middle, order[i - 1])
+            else:
+                if order[i - 1] < PASSED and i > 0:
+                    both(middle, order[i - 1])
+                both(first, c)
+                both(middle, c)
+            if i > 1:
+                second(order[i - 2])
+        second(LIFTED)
         second(LAST)
         arrived(back.at[1], b_recv.at[0])
         finish()
         sent(rows.at[0, 0, 0:2], pay_send.at[0])
-        sent(passed.at[0 : CHUNKS - 1], r_send.at[0])
         sent(crossed, r_send.at[1])
         sent(done.at[1:CHUNKS], b_send.at[0])
 
@@ -348,13 +353,20 @@
 
         def share(c, h):
             ref = parts.at[c, h]
-            for k, step in enumerate((1, 3)):
-                span = pl.ds(k * QUARTER // 2, QUARTER // 2)
-                dev = line_devs[h][2 if is_last(c) else step]
-                remote(band(ref, h, here[h][2], span), turned.at[c, h, k], p_send.at[0], p_recv.at[c, h], 2, dev).start()
-                if is_last(c):
-                    src = band(ref, h, here[h][step])
-                    remote(src, passed.at[c, h, 1 - k], p_send.at[2], r_recv.at[c, h], 2, line_devs[h][step]).start()
+
+            def send(straight):
+                for k, step in enumerate((1, 3)):
+                    src = band(ref, h, here[h][2], pl.ds(k * QUARTER // 2, QUARTER // 2))
+                    dev = line_devs[h][2 if straight else step]
+                    remote(src, turned.at[c, h, k], p_send.at[0], p_recv.at[c, h], 2, dev).start()
+                    if straight:
+                        src = band(ref, h, here[h][step])
+                        remote(src, passed.at[c, h, 1 - k], p_send.at[2], r_recv.at[c, h], 2, line_devs[h][step]).start()
+
+            if is_last(c):
+                send(True)
+            else:
+                send(True)
             remote(ref, ref, p_send.at[1], own_recv.at[c, h], 2, me).start()
 
         for c in range(DIRECT):
@@ -393,33 +405,36 @@
             made = jnp.concatenate([made[:, :, 0:QUARTER], made[:, :, QUARTER:HALF]], axis=1)
             parts[c, h] = made.astype(BF16).reshape(4, 4, 2 * ROW, QUARTER)
 
-        def batch(c, carry):
+        def batch(i, carry):
+            c = jnp.where(i < LAST, i, LIFTED)
+            after = jnp.where(i < LAST - 1, i + 1, jnp.where(i < LAST, LIFTED, LAST))
+
+            @pl.when(i + 3 < DIRECT)
+            def _():
+                widen(jnp.minimum(i + 3, DIRECT - 1), 1)
+
             lift()
 
-            @pl.when(c + 3 < DIRECT)
+            @pl.when(i + 2 < DIRECT)
             def _():
-                widen(jnp.minimum(c + 3, DIRECT - 1), 1)
+                widen(jnp.minimum(i + 2, DIRECT - 1), 2)
 
             lower(c, 0)
             share(c, 0)
 
-            @pl.when(c + 2 < DIRECT)
-            def _():
-                widen(jnp.minimum(c + 2, DIRECT - 1), 2)
-
-            @pl.when(c + 1 == SECOND)
+            @pl.when(i + 1 == SECOND)
             def _():
                 landed(SECOND, 1, True)
 
-            @pl.when((c + 1 > SECOND) & (c + 1 < DIRECT))
+            @pl.when((i + 1 > SECOND) & (i != LAST - 1))
             def _():
-                landed(jnp.minimum(c + 1, DIRECT - 1), 2, False)
-
-            @pl.when(c + 1 >= DIRECT)
+                landed(jnp.minimum(after, LAST), 2, False)
+
+            @pl.when(i == LAST - 1)
             def _():
-                arrived(rows.at[jnp.maximum(c + 1, DIRECT)], g_recv.at[jnp.maximum(c + 1, DIRECT), 2])
-
-            unfold(c + 1)
+                arrived(rows.at[LIFTED], g_recv.at[LIFTED, 2])
+
+            unfold(after)
             lower(c, 1)
             share(c, 1)
             return carry
@@ -437,7 +452,7 @@
         sent(rows.at[SECOND, 0:3], g_send.at[2])
         sent(turned, p_send.at[0])
         sent(parts, p_send.at[1])
-        sent(passed.at[LAST], p_send.at[2])
+        sent(passed.at[PASSED:CHUNKS], p_send.at[2])
 
 
 def local(

time: 67.2 us -> 63.7 us (0.948)
  the two profiles are of different devices: /device:TPU:0 before, /device:TPU:1 now
where the time goes in v4:
time: 63.7 us; the launch traced here: 63.5 us
  Pallas kernels  62 us (97%)
  local copies, waits for them, and re-layouts  1.47 us (2%)
    pallas_call x1, Pallas kernels, local(): pl.pallas_call(kernel, out_shape=jax.ShapeDtypeStruct(query.shape, BF16),...  62 us
    unnamed x1, local copies, waits for them, and re-layouts  1.47 us

profile of v4, /device:TPU:1, one launch (start us, length us, event | category | flops | bytes accessed | tf_op | source)
XLA Modules:
  0.0 63.5 jit_solution(11585338044117853270)
XLA Ops:
  0.0 62.0 %moe_block.1 = bf16[1,1,8,4096]{3,2,1,0:T(8,128)(2,1)} custom-call(bf16[1,1,8,4096]{3,2,1,0:T(8,128)(2,1)} %q.1, bf16[1,1,8,1024]{3,2,1,0:T(8,128)(2,1)} %nk.1, bf16[1,1,8,1024]{3,2,1,0:T(8,128)(2,1)} %nv.1, bf16[1,1,8,128,1024]{4,3,2,1,0:T(8,128)(2,1)} %ck.1, bf16[1,1,8,128,1024]{4,3,2,1,0:T(8,128)(2,1)} %cv.1, s32[1,1,8]{2,1,0:T(1,128)} %lengths.1, ...), custom_call_target="tpu_custom_call" | custom-call | tf_op jit(solution)/shard_map/moe_block/pallas_call | solution.py:468
  62.1 1.5 %copy.16 = bf16[1,1,8,4096]{3,2,1,0:T(8,128)(2,1)} copy(bf16[1,1,8,4096]{3,2,1,0:T(8,128)(2,1)} %moe_block.1) | data formatting | bytes 131072

commit v5 on v4

--- a/solution.py
+++ b/solution.py
@@ -277,7 +277,7 @@
             return parts.at[c, h, j, i] if h == 0 else parts.at[c, h, i, j]
 
         def first(c, h):
-            arrived(parts.at[c, h], own_recv.at[c, h])
+            arrived(band(parts.at[c, h], h, here[h][0]), own_recv.at[c, h])
             arrived(turned.at[c, h], p_recv.at[c, h])
             if c >= PASSED:
                 return
@@ -367,7 +367,8 @@
                 send(True)
             else:
                 send(True)
-            remote(ref, ref, p_send.at[1], own_recv.at[c, h], 2, me).start()
+            own = band(ref, h, here[h][0])
+            remote(own, own, p_send.at[1], own_recv.at[c, h], 2, me).start()
 
         for c in range(DIRECT):
             arrived(rows.at[c, y, x], pay_recv.at[c])
@@ -451,7 +452,7 @@
         sent(rows.at[2:DIRECT, 0:3], g_send.at[1])
         sent(rows.at[SECOND, 0:3], g_send.at[2])
         sent(turned, p_send.at[0])
-        sent(parts, p_send.at[1])
+        sent(turned, p_send.at[1])
         sent(passed.at[PASSED:CHUNKS], p_send.at[2])
 
 

time: 63.7 us -> 63.8 us (level)
  no operation moved by 1% of the time
where the time goes in v5:
time: 63.8 us; the launch traced here: 63.6 us
  Pallas kernels  62.1 us (97%)
  local copies, waits for them, and re-layouts  1.47 us (2%)
    pallas_call x1, Pallas kernels, local(): pl.pallas_call(kernel, out_shape=jax.ShapeDtypeStruct(query.shape, BF16),...  62.1 us
    unnamed x1, local copies, waits for them, and re-layouts  1.47 us

profile of v5, /device:TPU:1, one launch (start us, length us, event | category | flops | bytes accessed | tf_op | source)
XLA Modules:
  0.0 63.6 jit_solution(12476134957292408481)
XLA Ops:
  0.0 62.1 %moe_block.1 = bf16[1,1,8,4096]{3,2,1,0:T(8,128)(2,1)} custom-call(bf16[1,1,8,4096]{3,2,1,0:T(8,128)(2,1)} %q.1, bf16[1,1,8,1024]{3,2,1,0:T(8,128)(2,1)} %nk.1, bf16[1,1,8,1024]{3,2,1,0:T(8,128)(2,1)} %nv.1, bf16[1,1,8,128,1024]{4,3,2,1,0:T(8,128)(2,1)} %ck.1, bf16[1,1,8,128,1024]{4,3,2,1,0:T(8,128)(2,1)} %cv.1, s32[1,1,8]{2,1,0:T(1,128)} %lengths.1, ...), custom_call_target="tpu_custom_call" | custom-call | tf_op jit(solution)/shard_map/moe_block/pallas_call | solution.py:469
  62.1 1.5 %copy.16 = bf16[1,1,8,4096]{3,2,1,0:T(8,128)(2,1)} copy(bf16[1,1,8,4096]{3,2,1,0:T(8,128)(2,1)} %moe_block.1) | data formatting | bytes 131072
